TPU v7x, 32 devices: a whole 2x2x4 slice. The times are simulated.
32 devices in a mesh: dp: 4 (over y, x), seq: 8 (over z, core).
Axes of the slice: x: 2, y: 2, z: 4, core: 2. Of those that a mesh axis runs over, the one named last changes fastest.
Arguments:
- tokens: bfloat16 [4, 4096, 1024], P('dp', 'seq'), may hold values from -6 to 6
- starts: int32 [4, 13], P('dp'), may hold values from 0 to 4048, as said below
- query_key_value_weight: bfloat16 [1024, 3072], P(('dp', 'seq')), may hold values from -0.1875 to 0.1875
- attention_output_weight: bfloat16 [1024, 1024], P(('dp', 'seq')), may hold values from -0.75 to 0.75
- up_projection_weight: bfloat16 [1024, 4096], P(('dp', 'seq')), may hold values from -0.1875 to 0.1875
- down_projection_weight: bfloat16 [4096, 1024], P(('dp', 'seq')), may hold values from -0.09375 to 0.09375
- first_gain: bfloat16 [1024], P(('dp', 'seq')), may hold values from 0.5 to 1.5
- first_shift: bfloat16 [1024], P(('dp', 'seq')), may hold values from -0.5 to 0.5
- second_gain: bfloat16 [1024], P(('dp', 'seq')), may hold values from 0.5 to 1.5
- second_shift: bfloat16 [1024], P(('dp', 'seq')), may hold values from -0.5 to 0.5
- cotangent: bfloat16 [4, 4096, 1024], P('dp', 'seq'), may hold values from -6 to 6
Outputs:
- result_tokens: bfloat16 [4, 4096, 1024], P('dp', 'seq')
- grad_tokens: float32 [4, 4096, 1024], P('dp', 'seq')
- grad_input_weight: float32 [1024, 3072], P(('dp', 'seq'))
- grad_output_weight: float32 [1024, 1024], P(('dp', 'seq'))
- grad_upward_weight: float32 [1024, 4096], P(('dp', 'seq'))
- grad_downward_weight: float32 [4096, 1024], P(('dp', 'seq'))
- grad_first_gain: float32 [1024], P(('dp', 'seq'))
- grad_first_shift: float32 [1024], P(('dp', 'seq'))
- grad_second_gain: float32 [1024], P(('dp', 'seq'))
- grad_second_shift: float32 [1024], P(('dp', 'seq'))
Inputs may be any that keep to these rules, and one draw needn't show every extreme that they name: In each packed sequence starts[0] = 0 and the first image holds 64 positions; the other 12 images follow back to end, 4 of 768 positions, 4 of 192 and 4 of 48, in an order drawn from the seed except that the last is always one of 48 positions; the last ends at the sequence's end.
All inputs are finite; a program needn't handle non-finite values.
Results may differ from a plain program's by a relative error of at most 0.008.
Values may be sent and summed in bfloat16 or wider, within the bound.
A program may use at most 192 MiB of HBM per device.

v0:
```python
import jax
import jax.numpy as jnp
from jax import lax
from jax.sharding import PartitionSpec as P

HEAD = 64
BLOCK = 512


def prefix(value, axis, combine, identity, reverse):
    size, mine = (lax.axis_size(axis), lax.axis_index(axis))
    everything = jax.tree.map(
        lambda part, kind: lax.all_gather(part.astype(kind), axis),
        value,
        jax.tree.map(lambda a: jnp.bfloat16 if a.dtype == jnp.float32 else a.dtype, value),
    )
    start = jax.tree.map(
        lambda part, zero: jnp.broadcast_to(jnp.asarray(zero, part.dtype), part.shape),
        value,
        identity,
    )

    def lap(k, before):
        at = size - 1 - k if reverse else k
        reached = at > mine if reverse else at < mine
        new = combine(
            before, jax.tree.map(lambda part, own: part[at].astype(own.dtype), everything, value)
        )
        return jax.tree.map(lambda a, b: jnp.where(reached, a, b), new, before)

    return lax.fori_loop(0, size, lap, start)


def layer_norm(values, norm_gain, norm_shift):
    average = jnp.mean(values, axis=-1, keepdims=True)
    centred = values - average
    spread = jnp.mean(centred * centred, axis=-1, keepdims=True)
    return centred * lax.rsqrt(spread + 1e-05) * norm_gain + norm_shift


def feature(values):
    return jax.nn.elu(values) + 1.0


def combine(former, latter):
    return (
        former[0] * latter[0],
        latter[0] * former[1] + latter[1],
        latter[0] * former[2] + latter[2],
    )


def rows_product(factor_one, factor_two):
    return lax.dot_general(
        factor_one, factor_two, (((0,), (0,)), ((), ())), preferred_element_type=jnp.float32
    )


def cols_product(factor_one, factor_two):
    return lax.dot_general(
        factor_one, factor_two, (((1,), (1,)), ((), ())), preferred_element_type=jnp.float32
    )


def on_device(
    tokens,
    starts,
    query_key_value_weight,
    attention_output_weight,
    up_projection_weight,
    down_projection_weight,
    first_gain,
    first_shift,
    second_gain,
    second_shift,
    cotangent,
):
    local_len = tokens.shape[1]
    model_width = tokens.shape[2]
    head_count = model_width // HEAD
    block_count = local_len // BLOCK
    block_shape = (block_count, BLOCK, head_count, HEAD)
    zero_low = jnp.zeros((), jnp.bfloat16)
    input_tokens = tokens[0].astype(jnp.float32)
    first_pos = lax.axis_index("seq") * local_len
    positions = first_pos + jnp.arange(local_len, dtype=jnp.int32)
    pack_starts = starts[0]
    image_ids = jnp.sum((pack_starts[None, :] <= positions[:, None]).astype(jnp.int32), axis=1) - 1
    before_id = jnp.sum((pack_starts <= first_pos - 1).astype(jnp.int32)) - 1
    causal = jnp.arange(BLOCK)[:, None] >= jnp.arange(BLOCK)[None, :]
    attn_set = (
        lax.all_gather(query_key_value_weight, ("dp", "seq"), axis=0, tiled=True),
        lax.all_gather(attention_output_weight, ("dp", "seq"), axis=0, tiled=True),
        lax.all_gather(first_gain, ("dp", "seq"), axis=0, tiled=True),
        lax.all_gather(first_shift, ("dp", "seq"), axis=0, tiled=True),
    )
    in_full = attn_set[0]
    out_full = attn_set[1]
    gain_one = attn_set[2].astype(jnp.float32)
    shift_one = attn_set[3].astype(jnp.float32)
    first_normed_tokens = layer_norm(input_tokens, gain_one, shift_one)
    normed_low = first_normed_tokens.astype(jnp.bfloat16)
    projected_tokens = jnp.dot(normed_low, in_full, preferred_element_type=jnp.float32)
    queries = projected_tokens[:, :model_width]
    keys_raw = projected_tokens[:, model_width : 2 * model_width]
    values_raw = projected_tokens[:, 2 * model_width :]
    feat_query = feature(queries).astype(jnp.bfloat16).reshape(block_shape)
    feat_key = feature(keys_raw).astype(jnp.bfloat16).reshape(block_shape)
    value_low = values_raw.astype(jnp.bfloat16).reshape(block_shape)
    block_number = 0
    last_id = image_ids[-1]
    tail_mask = image_ids == last_id
    tail_key = jnp.where(tail_mask[:, None, None], feat_key[block_number], zero_low)
    keep_list = [image_ids == before_id]
    tail_list = [tail_mask]
    flag_list = [(last_id == before_id).astype(jnp.float32)]
    same_list = [causal & (image_ids[:, None] == image_ids[None, :])]
    update_list = [
        jnp.einsum(
            "jhe,jhf->hef", tail_key, value_low[block_number], preferred_element_type=jnp.float32
        )
    ]
    total_list = [jnp.sum(tail_key.astype(jnp.float32), axis=0)]
    identity = (
        jnp.ones((), jnp.float32),
        jnp.zeros((head_count, HEAD, HEAD), jnp.float32),
        jnp.zeros((head_count, HEAD), jnp.float32),
    )
    combined = identity
    block_number = 0
    combined = combine(
        combined, (flag_list[block_number], update_list[block_number], total_list[block_number])
    )
    entering = prefix(combined, "seq", combine, identity, False)
    memory = entering[1]
    key_sum = entering[2]
    block_number = 0
    query_block = feat_query[block_number]
    keep_float = keep_list[block_number].astype(jnp.float32)
    memory_low = memory.astype(jnp.bfloat16)
    raw_scores = jnp.einsum(
        "the,jhe->htj", query_block, feat_key[block_number], preferred_element_type=jnp.float32
    )
    masked = jnp.where(same_list[block_number][None], raw_scores, 0.0)
    scores_low = masked.astype(jnp.bfloat16)
    carried = (
        jnp.einsum("the,hef->thf", query_block, memory_low, preferred_element_type=jnp.float32)
        * keep_float[:, None, None]
    )
    numerator = (
        jnp.einsum(
            "htj,jhf->thf", scores_low, value_low[block_number], preferred_element_type=jnp.float32
        )
        + carried
    )
    denominator = jnp.transpose(jnp.sum(masked, axis=2)) + keep_float[:, None] * jnp.sum(
        query_block.astype(jnp.float32) * key_sum[None], axis=2
    )
    memory_list = [memory_low]
    keysum_list = [key_sum]
    numer_list = [numerator]
    denom_list = [denominator]
    ratio_list = numerator / denominator[:, :, None]
    mixed_low = ratio_list.reshape(local_len, model_width).astype(jnp.bfloat16)
    middle_tokens = input_tokens + jnp.dot(mixed_low, out_full, preferred_element_type=jnp.float32)
    mlp_set = (
        lax.all_gather(up_projection_weight, ("dp", "seq"), axis=0, tiled=True),
        lax.all_gather(down_projection_weight, ("dp", "seq"), axis=0, tiled=True),
        lax.all_gather(second_gain, ("dp", "seq"), axis=0, tiled=True),
        lax.all_gather(second_shift, ("dp", "seq"), axis=0, tiled=True),
    )
    up_full = mlp_set[0]
    down_full = mlp_set[1]
    gain_two = mlp_set[2].astype(jnp.float32)
    shift_two = mlp_set[3].astype(jnp.float32)
    normed_two_low = layer_norm(middle_tokens, gain_two, shift_two).astype(jnp.bfloat16)
    upper_hidden = jnp.dot(normed_two_low, up_full, preferred_element_type=jnp.float32)
    active_low = jax.nn.gelu(upper_hidden).astype(jnp.bfloat16)
    result = middle_tokens + jnp.dot(active_low, down_full, preferred_element_type=jnp.float32)
    result_tokens = result.astype(jnp.bfloat16).reshape(1, local_len, model_width)
    grad_out = cotangent[0].astype(jnp.float32)
    mlp_again = (
        lax.all_gather(up_projection_weight, ("dp", "seq"), axis=0, tiled=True),
        lax.all_gather(down_projection_weight, ("dp", "seq"), axis=0, tiled=True),
        lax.all_gather(second_gain, ("dp", "seq"), axis=0, tiled=True),
        lax.all_gather(second_shift, ("dp", "seq"), axis=0, tiled=True),
    )
    up_back = mlp_again[0]
    down_back = mlp_again[1]
    grad_out_low = cotangent[0]
    grad_down = rows_product(active_low, grad_out_low)
    d_active = cols_product(grad_out_low, down_back)
    gelu_value, gelu_back = jax.vjp(jax.nn.gelu, upper_hidden)
    g_upper = gelu_back(d_active)[0].astype(jnp.bfloat16)
    grad_up = rows_product(normed_two_low, g_upper)
    d_normed_two = cols_product(g_upper, up_back)
    norm_value, norm_back = jax.vjp(layer_norm, middle_tokens, gain_two, shift_two)
    middle_part, grad_gain_two, grad_shift_two = norm_back(d_normed_two)
    g_middle = grad_out + middle_part
    attn_again = (
        lax.all_gather(query_key_value_weight, ("dp", "seq"), axis=0, tiled=True),
        lax.all_gather(attention_output_weight, ("dp", "seq"), axis=0, tiled=True),
        lax.all_gather(first_gain, ("dp", "seq"), axis=0, tiled=True),
        lax.all_gather(first_shift, ("dp", "seq"), axis=0, tiled=True),
    )
    in_back = attn_again[0]
    out_back = attn_again[1]
    g_middle_low = g_middle.astype(jnp.bfloat16)
    grad_out_weight = rows_product(mixed_low, g_middle_low)
    d_mixed = cols_product(g_middle_low, out_back).reshape(block_shape)
    block_number = 0
    query_block = feat_query[block_number]
    denominator = denom_list[block_number]
    g_numerator = (d_mixed[block_number] / denominator[:, :, None]).astype(jnp.bfloat16)
    g_denominator = -jnp.sum(d_mixed[block_number] * numer_list[block_number], axis=2) / (
        denominator * denominator
    )
    kept_query = jnp.where(keep_list[block_number][:, None, None], query_block, zero_low)
    gnum_list = [g_numerator]
    gden_list = [g_denominator]
    local_list = [
        jnp.einsum("the,thf->hef", kept_query, g_numerator, preferred_element_type=jnp.float32)
    ]
    localkey_list = [jnp.sum(kept_query.astype(jnp.float32) * g_denominator[:, :, None], axis=0)]
    combined = identity
    for block_number in reversed(range(block_count)):
        combined = combine(
            combined,
            (flag_list[block_number], local_list[block_number], localkey_list[block_number]),
        )
    leaving = prefix(combined, "seq", combine, identity, True)
    g_memory = leaving[1]
    g_key_sum = leaving[2]
    gq_list = []
    gk_list = []
    gv_list = []
    for block_number in reversed(range(block_count)):
        query_block = feat_query[block_number]
        key_block = feat_key[block_number]
        value_block = value_low[block_number]
        keep_float = keep_list[block_number].astype(jnp.float32)
        tail_float = tail_list[block_number].astype(jnp.float32)
        g_numerator = gnum_list[block_number]
        g_denominator = gden_list[block_number]
        g_update = g_memory.astype(jnp.bfloat16)
        raw_scores = jnp.einsum(
            "the,jhe->htj", query_block, key_block, preferred_element_type=jnp.float32
        )
        scores_low = jnp.where(same_list[block_number][None], raw_scores, 0.0).astype(jnp.bfloat16)
        g_scores = (
            jnp.einsum("thf,jhf->htj", g_numerator, value_block, preferred_element_type=jnp.float32)
            + jnp.transpose(g_denominator)[:, :, None]
        )
        g_scores_low = jnp.where(
            same_list[block_number][None], g_scores.astype(jnp.bfloat16), zero_low
        )
        query_grad = jnp.einsum(
            "htj,jhe->the", g_scores_low, key_block, preferred_element_type=jnp.float32
        )
        query_grad = query_grad + keep_float[:, None, None] * (
            jnp.einsum(
                "thf,hef->the",
                g_numerator,
                memory_list[block_number],
                preferred_element_type=jnp.float32,
            )
            + g_denominator[:, :, None] * keysum_list[block_number][None]
        )
        key_grad = jnp.einsum(
            "htj,the->jhe", g_scores_low, query_block, preferred_element_type=jnp.float32
        )
        key_grad = key_grad + tail_float[:, None, None] * (
            jnp.einsum("jhf,hef->jhe", value_block, g_update, preferred_element_type=jnp.float32)
            + g_key_sum[None]
        )
        tail_key = jnp.where(tail_list[block_number][:, None, None], key_block, zero_low)
        value_grad = jnp.einsum(
            "htj,thf->jhf", scores_low, g_numerator, preferred_element_type=jnp.float32
        )
        value_grad = value_grad + jnp.einsum(
            "jhe,hef->jhf", tail_key, g_update, preferred_element_type=jnp.float32
        )
        gq_list.append(query_grad)
        gk_list.append(key_grad)
        gv_list.append(value_grad)
        g_memory = local_list[block_number] + flag_list[block_number] * g_memory
        g_key_sum = localkey_list[block_number] + flag_list[block_number] * g_key_sum
    d_feat_query = jnp.concatenate(gq_list[::-1], axis=0).reshape(local_len, model_width)
    d_feat_key = jnp.concatenate(gk_list[::-1], axis=0).reshape(local_len, model_width)
    d_value = jnp.concatenate(gv_list[::-1], axis=0).reshape(local_len, model_width)
    query_value, query_back = jax.vjp(feature, queries)
    key_value, key_back = jax.vjp(feature, keys_raw)
    g_projected = jnp.concatenate(
        [query_back(d_feat_query)[0], key_back(d_feat_key)[0], d_value], axis=1
    ).astype(jnp.bfloat16)
    grad_in_weight = rows_product(normed_low, g_projected)
    d_normed = cols_product(g_projected, in_back)
    first_value, first_back = jax.vjp(layer_norm, input_tokens, gain_one, shift_one)
    input_part, grad_gain_one, grad_shift_one = first_back(d_normed)
    grad_tokens = (g_middle + input_part).reshape(1, local_len, model_width)
    summed = (
        lax.psum_scatter(grad_in_weight, ("dp", "seq"), scatter_dimension=0, tiled=True),
        lax.psum_scatter(grad_out_weight, ("dp", "seq"), scatter_dimension=0, tiled=True),
        lax.psum_scatter(grad_up, ("dp", "seq"), scatter_dimension=0, tiled=True),
        lax.psum_scatter(grad_down, ("dp", "seq"), scatter_dimension=0, tiled=True),
        lax.psum_scatter(grad_gain_one, ("dp", "seq"), scatter_dimension=0, tiled=True),
        lax.psum_scatter(grad_shift_one, ("dp", "seq"), scatter_dimension=0, tiled=True),
        lax.psum_scatter(grad_gain_two, ("dp", "seq"), scatter_dimension=0, tiled=True),
        lax.psum_scatter(grad_shift_two, ("dp", "seq"), scatter_dimension=0, tiled=True),
    )
    return (
        result_tokens,
        grad_tokens,
        summed[0],
        summed[1],
        summed[2],
        summed[3],
        summed[4],
        summed[5],
        summed[6],
        summed[7],
    )


def solution(mesh):
    return jax.shard_map(
        on_device,
        mesh=mesh,
        in_specs=(
            P("dp", "seq", None),
            P("dp", None),
            P(("dp", "seq"), None),
            P(("dp", "seq"), None),
            P(("dp", "seq"), None),
            P(("dp", "seq"), None),
            P(("dp", "seq")),
            P(("dp", "seq")),
            P(("dp", "seq")),
            P(("dp", "seq")),
            P("dp", "seq", None),
        ),
        out_specs=(
            P("dp", "seq", None),
            P("dp", "seq", None),
            P(("dp", "seq"), None),
            P(("dp", "seq"), None),
            P(("dp", "seq"), None),
            P(("dp", "seq"), None),
            P(("dp", "seq")),
            P(("dp", "seq")),
            P(("dp", "seq")),
            P(("dp", "seq")),
        ),
        check_vma=False,
    )
```

profile of v0, /device:TPU:0, one launch (start us, length us, event | category | flops | bytes accessed | tf_op | source)
XLA Modules:
  0.0 1083.8 jit_solution(13893049380607313941)
XLA Ops:
  11.3 42.6 %all-reduce.10 = (bf16[1024]{0:T(1024)(128)(2,1)S(1)}, bf16[1024]{0:T(1024)(128)(2,1)S(1)}, bf16[1024]{0:T(1024)(128)(2,1)S(1)}, bf16[1024]{0:T(1024)(128)(2,1)S(1)}) all-reduce(bf16[1024]{0:T(1024)(128)(2,1)S(1)} %dynamic-update-slice.1, bf16[1024]{0:T(1024)(128)(2,1)S(1)} %dynamic-update-slice, ...), channel_id=1, replica_groups=mesh['dp'=4,'seq'=8] {'dp','seq'}, use_global_device_ids=true, to_apply=%add.1 | all-reduce | flops 4096 | bytes 16384
  58.6 2.0 fusion.28
  61.8 21.7 %all-gather.9.cloned.1.call-done = bf16[1024,3072]{1,0:T(8,128)(2,1)} async-done(((bf16[32,3072]{1,0:T(8,128)(2,1)}), bf16[1024,3072]{1,0:T(8,128)(2,1)}) %all-gather.9.cloned.1.call-update) | async-done | bytes 6291472 | tf_op jit(solution)/shard_map/all_gather | solution.py:92
  83.5 5.8 fusion.76
  89.3 2.6 copy-done.1
  91.9 2.1 select_reduce_fusion.1
  94.6 1.9 copy.79
  101.6 15.7 %all-reduce.2 = bf16[8]{0:T(256)(128)(2,1)S(1)} all-reduce(bf16[8]{0:T(256)(128)(2,1)S(1)} %dynamic-update-slice.2), channel_id=1, replica_groups=mesh['dp'=4,'seq'=8] {'seq'}, use_global_device_ids=true, to_apply=%add.2 | all-reduce | flops 8 | bytes 32
  118.2 3.5 fusion.39
  121.6 2.3 copy.80
  124.0 14.2 %all_gather.63 = bf16[8,16,64]{2,1,0:T(8,128)(2,1)S(1)} all-gather(bf16[1,16,64]{2,1,0:T(8,128)(2,1)S(1)} %convert_element_type.222), channel_id=1, replica_groups=mesh['dp'=4,'seq'=8] {'seq'}, dimensions={0}, use_global_device_ids=true | all-gather | bytes 18432 | tf_op jit(solution)/shard_map/all_gather | solution.py:13
  138.2 4.0 select_reduce_fusion
  142.3 3.2 copy-done.49
  145.5 3.0 fusion.16
  148.4 20.6 %while.34 = (s32[]{:T(128)}, f32[16,64,64]{2,1,0:T(8,128)S(1)}, f32[16,64]{1,0:T(8,128)S(1)}, s32[]{:T(128)}, bf16[8]{0:T(256)(128)(2,1)S(1)}, /*index=5*/bf16[8...) while((s32[]{:T(128)}, f32[16,64,64]{2,1,0:T(8,128)S(1)}, ...), condition=%wide.region_6.7_spmd.clone, body=%wide.region_5.6_spmd.clone.sunk | while | flops 332805 | bytes 665753 | solution.py:31
  170.0 3.8 fusion.32
  173.8 11.0 %all-gather.11.cloned.1.call-done = bf16[1024,1024]{1,0:T(8,128)(2,1)} async-done(((bf16[32,1024]{1,0:T(8,128)(2,1)}), bf16[1024,1024]{1,0:T(8,128)(2,1)}) %all-gather.11.cloned.1.call-update) | async-done | bytes 2097168 | tf_op jit(solution)/shard_map/all_gather | solution.py:93
  184.7 3.3 fusion.86
  189.7 74.0 %all-gather.13.cloned.1.call-done = bf16[1024,4096]{1,0:T(8,128)(2,1)} async-done(((bf16[32,4096]{1,0:T(8,128)(2,1)}), bf16[1024,4096]{1,0:T(8,128)(2,1)}) %all-gather.13.cloned.1.call-update) | async-done | bytes 8388624 | tf_op jit(solution)/shard_map/all_gather | solution.py:167
  263.7 11.8 %fusion.80 = f32[512,4096]{1,0:T(8,128)} fusion(bf16[1024,4096]{1,0:T(8,128)(2,1)} %all-gather.13.cloned.1.call-done, f32[512,1024]{1,0:T(8,128)} %copy-done.4, f32[1024]{0:T(1024)S(1)} %copy-done.40, f32[1024]{0:T(1024)S(1)} %convert_element_type.228, f32[512]{0:T(512)S(1)} %fusion.64, f32[512]{0:T(512)S(1)} %broadcast_multiply_fusion), kind=kOutput, calls=%fused_computation.137 | convolution fusion | flops 4297588736 | bytes 18886656 | tf_op jit(solution)/shard_map/dot_general | solution.py:177
  275.6 67.0 %all-gather.15.cloned.1.call-done = bf16[4096,1024]{1,0:T(8,128)(2,1)} async-done(((bf16[128,1024]{1,0:T(8,128)(2,1)}), bf16[4096,1024]{1,0:T(8,128)(2,1)}) %all-gather.15.cloned.1.call-update) | async-done | bytes 8388624 | tf_op jit(solution)/shard_map/all_gather | solution.py:168
  342.6 13.0 %fusion.10 = bf16[512,4096]{1,0:T(8,128)(2,1)S(1)} fusion(f32[512,4096]{1,0:T(8,128)} %fusion.80, bf16[4096,1024]{1,0:T(8,128)(2,1)} %all-gather.15.cloned.1.call-done, bf16[1,512,1024]{2,1,0:T(8,128)(2,1)S(1)} %copy-done.20), kind=kOutput, calls=%fused_computation.19 | convolution fusion | flops 4336910336 | bytes 22020096 | tf_op jit(solution)/shard_map/dot_general | solution.py:60
  355.7 5.5 multiply_reduce_fusion
  371.3 2.9 copy.90
  374.2 3.6 multiply_reduce_fusion.1
  380.5 3.3 fusion.87
  383.8 6.9 add_convert_fusion
  391.5 7.3 fusion.31
  398.8 2.9 copy.87
  401.7 14.0 %all_gather.71 = bf16[8,16,64]{2,1,0:T(8,128)(2,1)S(1)} all-gather(bf16[1,16,64]{2,1,0:T(8,128)(2,1)S(1)} %convert_element_type.242), channel_id=1, replica_groups=mesh['dp'=4,'seq'=8] {'seq'}, dimensions={0}, use_global_device_ids=true | all-gather | bytes 18432 | tf_op jit(solution)/shard_map/all_gather | solution.py:13
  415.7 7.4 fusion.15
  423.1 7.4 fusion.11
  430.5 20.6 %while.35 = (s32[]{:T(128)}, f32[16,64,64]{2,1,0:T(8,128)S(1)}, f32[16,64]{1,0:T(8,128)S(1)}, s32[]{:T(128)}, bf16[8]{0:T(256)(128)(2,1)S(1)}, /*index=5*/bf16[8...) while((s32[]{:T(128)}, f32[16,64,64]{2,1,0:T(8,128)S(1)}, ...), condition=%wide.region_16.17_spmd.clone, body=%wide.region_15.16_spmd.clone.sunk | while | flops 332809 | bytes 665815 | solution.py:31
  451.2 3.0 add_convert_fusion.1
  454.3 2.4 copy.95
  456.6 3.3 multiply_add_fusion
  460.0 3.1 copy.91
  463.1 4.3 add_convert_fusion.3
  468.7 7.1 fusion.42
  477.3 10.5 fusion.79
  488.1 15.2 %fusion.44 = f32[4096,1024]{1,0:T(8,128)} fusion(bf16[1,512,1024]{2,1,0:T(8,128)(2,1)} %param.25, f32[512,4096]{1,0:T(8,128)} %fusion.80), kind=kOutput, calls=%fused_computation.85 | convolution fusion | flops 4313841664 | bytes 26214400 | tf_op jit(solution)/shard_map/dot_general | solution.py:54
  503.4 12.1 %fusion.40 = bf16[1,512,1024]{2,1,0:T(8,128)(2,1)} fusion(f32[512,1024]{1,0:T(8,128)S(1)} %copy-done.6, bf16[4096,1024]{1,0:T(8,128)(2,1)} %all-gather.15.cloned.1.call-done, f32[512,4096]{1,0:T(8,128)} %fusion.80), kind=kOutput, calls=%fused_computation.79 | convolution fusion | flops 4314890240 | bytes 19922944 | tf_op jit(solution)/shard_map/dot_general | solution.py:179
  515.5 6.8 fusion.81
  524.6 38.0 %all-reduce.9 = (f32[1024]{0:T(1024)S(1)}, f32[1024]{0:T(1024)S(1)}, f32[1024]{0:T(1024)S(1)}, f32[1024]{0:T(1024)S(1)}) all-reduce(f32[1024]{0:T(1024)S(1)} %get-tuple-element.366, f32[1024]{0:T(1024)S(1)} %get-tuple-element.369, f32[1024]{0:T(1024)S(1)} %copy-done.42, ...), channel_id=8, replica_groups=mesh['dp'=4,'seq'=8] {'dp','seq'}, use_global_device_ids=true, to_apply=%region_24.25.clone | all-reduce | flops 4096 | bytes 32768
  565.0 4.3 add_bitcast_fusion
  569.3 131.3 %reduce-scatter.5.cloned.1.call-done = f32[32,3072]{1,0:T(8,128)} async-done(((f32[1024,3072]{1,0:T(8,128)}), f32[32,3072]{1,0:T(8,128)}) %reduce-scatter.5.cloned.1.call-update) | async-done | bytes 393232 | tf_op jit(solution)/shard_map/reduce_scatter | solution.py:302
  700.5 188.8 %reduce-scatter.9.cloned.1.call-done = f32[32,4096]{1,0:T(8,128)} async-done(((f32[1024,4096]{1,0:T(8,128)}), f32[32,4096]{1,0:T(8,128)}) %reduce-scatter.9.cloned.1.call-update) | async-done | bytes 524304 | tf_op jit(solution)/shard_map/reduce_scatter | solution.py:304
  889.3 187.2 %reduce-scatter.11.cloned.1.call-done = f32[128,1024]{1,0:T(8,128)} async-done(((f32[4096,1024]{1,0:T(8,128)}), f32[128,1024]{1,0:T(8,128)}) %reduce-scatter.11.cloned.1.call-update) | async-done | bytes 524304 | tf_op jit(solution)/shard_map/reduce_scatter | solution.py:305
  (227 shorter events, 69.3 us)
Async XLA Ops:
  7.2 76.3 %copy-start = (bf16[1,512,1024]{2,1,0:T(8,128)(2,1)S(1)}, bf16[1,512,1024]{2,1,0:T(8,128)(2,1)}, u32[]{:S(2)}) copy-start(bf16[1,512,1024]{2,1,0:T(8,128)(2,1)} %param.15) | copy-start | bytes 3145732
  7.2 76.3 %all-gather.9.cloned.1.call-start = ((), (), s32[]{:S(2)}) async-start(), calls=%async_computation.4 | async-start | bytes 6488064 | tf_op jit(solution)/shard_map/all_gather | solution.py:92
  7.9 140.5 %all-gather.17.cloned.1.call-start = ((), (), s32[]{:S(2)}) async-start(), calls=%async_computation.12 | async-start | bytes 2359296 | tf_op jit(solution)/shard_map/all_gather | solution.py:13
  60.6 28.7 %copy-start.31 = (f32[512]{0:T(512)}, f32[512]{0:T(512)S(1)}, u32[]{:S(2)}) copy-start(f32[512]{0:T(512)S(1)} %fusion.28) | copy-start | bytes 6148
  61.8 34.6 %copy-start.38 = (pred[512]{0:T(512)(128)(4,1)}, pred[512]{0:T(512)(128)(4,1)S(1)}, u32[]{:S(2)}) copy-start(pred[512]{0:T(512)(128)(4,1)S(1)} %get-tuple-element.419) | copy-start | bytes 1540
  89.3 2.7 copy-start.1
  94.6 3.1 copy-start.16
  96.5 45.8 %copy-start.7 = (bf16[512,1024]{0,1:T(8,128)(2,1)}, bf16[512,1024]{0,1:T(8,128)(2,1)S(1)}, u32[]{:S(2)}) copy-start(bf16[512,1024]{0,1:T(8,128)(2,1)S(1)} %copy.79) | copy-start | bytes 3145732
  96.5 3.8 copy-start.48
  97.6 87.1 %all-gather.11.cloned.1.call-start = ((), (), s32[]{:S(2)}) async-start(), calls=%async_computation.5 | async-start | bytes 2162688 | tf_op jit(solution)/shard_map/all_gather | solution.py:93
  98.4 165.4 %all-gather.13.cloned.1.call-start = ((), (), s32[]{:S(2)}) async-start(), calls=%async_computation.6 | async-start | bytes 8650752 | tf_op jit(solution)/shard_map/all_gather | solution.py:167
  99.0 243.6 %all-gather.15.cloned.1.call-start = ((), (), s32[]{:S(2)}) async-start(), calls=%async_computation.7 | async-start | bytes 8650752 | tf_op jit(solution)/shard_map/all_gather | solution.py:168
  99.5 331.0 %all-gather.19.cloned.1.call-start = ((), (), s32[]{:S(2)}) async-start(), calls=%async_computation.13 | async-start | bytes 2359296 | tf_op jit(solution)/shard_map/all_gather | solution.py:13
  117.9 243.2 %copy-start.33 = (f32[1024]{0:T(1024)}, f32[1024]{0:T(1024)S(1)}, u32[]{:S(2)}) copy-start(f32[1024]{0:T(1024)S(1)} %convert_element_type.228) | copy-start | bytes 12292
  142.2 3.2 copy-start.49
  142.2 27.7 %copy-start.30 = (f32[16,512]{1,0:T(8,128)}, f32[16,512]{1,0:T(8,128)S(1)}, u32[]{:S(2)}) copy-start(f32[16,512]{1,0:T(8,128)S(1)} %get-tuple-element.420) | copy-start | bytes 98308
  148.4 21.1 %copy-start.21 = (bf16[512,1024]{0,1:T(8,128)(2,1)S(1)}, bf16[512,1024]{0,1:T(8,128)(2,1)}, u32[]{:S(2)}) copy-start(bf16[512,1024]{0,1:T(8,128)(2,1)} %copy.80) | copy-start | bytes 3145732
  188.0 75.7 %copy-start.40 = (f32[1024]{0:T(1024)S(1)}, f32[1024]{0:T(1024)}, u32[]{:S(2)}) copy-start(f32[1024]{0:T(1024)} %convert_element_type.229) | copy-start | bytes 12292
  189.7 171.5 %copy-start.35 = (f32[512]{0:T(512)}, f32[512]{0:T(512)S(1)}, u32[]{:S(2)}) copy-start(f32[512]{0:T(512)S(1)} %fusion.64) | copy-start | bytes 6148
  189.7 152.9 %copy-start.20 = (bf16[1,512,1024]{2,1,0:T(8,128)(2,1)S(1)}, bf16[1,512,1024]{2,1,0:T(8,128)(2,1)}, u32[]{:S(2)}) copy-start(bf16[1,512,1024]{2,1,0:T(8,128)(2,1)} %param.25) | copy-start | bytes 3145732
  342.6 13.0 %copy-start.5 = (f32[512,1024]{1,0:T(8,128)S(1)}, f32[512,1024]{1,0:T(8,128)}, u32[]{:S(2)}) copy-start(f32[512,1024]{1,0:T(8,128)} %copy-done.4) | copy-start | bytes 6291460
  342.6 13.1 %copy-start.45 = (bf16[1024,4096]{1,0:T(8,128)(2,1)S(1)}, bf16[1024,4096]{1,0:T(8,128)(2,1)}, u32[]{:S(2)}) copy-start(bf16[1024,4096]{1,0:T(8,128)(2,1)} %all-gather.13.cloned.1.call-done) | copy-start | bytes 25165828
  355.7 5.5 copy-start.50
  361.9 2.4 copy-start.9
  361.9 3.3 copy-start.26
  363.2 3.4 copy-start.24
  369.0 200.3 %reduce-scatter.7.cloned.1.call-start = ((), (), s32[]{:S(2)}) async-start(), calls=%async_computation.9 | async-start | bytes 4325376 | tf_op jit(solution)/shard_map/reduce_scatter | solution.py:303
  377.8 2.7 copy-start.25
  377.8 2.7 copy-start.27
  390.7 309.8 %reduce-scatter.5.cloned.1.call-start = ((), (), s32[]{:S(2)}) async-start(), calls=%async_computation.8 | async-start | bytes 12976128 | tf_op jit(solution)/shard_map/reduce_scatter | solution.py:302
  415.7 7.4 copy-start.23
  423.1 7.4 copy-start.47
  430.5 20.6 %copy-start.17 = (bf16[512,1024]{0,1:T(8,128)(2,1)S(1)}, bf16[512,1024]{0,1:T(8,128)(2,1)}, u32[]{:S(2)}) copy-start(bf16[512,1024]{0,1:T(8,128)(2,1)} %copy-done.16) | copy-start | bytes 3145732
  430.5 20.7 %copy-start.39 = (pred[512]{0:T(512)(128)(4,1)S(1)}, pred[512]{0:T(512)(128)(4,1)}, u32[]{:S(2)}) copy-start(pred[512]{0:T(512)(128)(4,1)} %copy-done.38) | copy-start | bytes 1540
  454.3 2.4 copy-start.8
  454.3 2.4 copy-start.37
  460.0 3.1 copy-start.10
  463.1 5.6 copy-start.18
  475.7 1.6 copy-start.41
  475.7 413.6 %reduce-scatter.9.cloned.1.call-start = ((), (), s32[]{:S(2)}) async-start(), calls=%async_computation.10 | async-start | bytes 17301504 | tf_op jit(solution)/shard_map/reduce_scatter | solution.py:304
  487.8 588.7 %reduce-scatter.11.cloned.1.call-start = ((), (), s32[]{:S(2)}) async-start(), calls=%async_computation.11 | async-start | bytes 17301504 | tf_op jit(solution)/shard_map/reduce_scatter | solution.py:305
  503.3 12.2 %copy-start.13 = (bf16[512,1024]{1,0:T(8,128)(2,1)S(1)}, bf16[512,1024]{1,0:T(8,128)(2,1)}, u32[]{:S(2)}) copy-start(bf16[512,1024]{1,0:T(8,128)(2,1)} %copy-done.12) | copy-start | bytes 3145732
  503.4 12.1 %copy-start.15 = (bf16[512,1024]{1,0:T(8,128)(2,1)S(1)}, bf16[512,1024]{1,0:T(8,128)(2,1)}, u32[]{:S(2)}) copy-start(bf16[512,1024]{1,0:T(8,128)(2,1)} %copy-done.14) | copy-start | bytes 3145732
  503.4 12.1 %copy-start.19 = (bf16[512,1024]{1,0:T(8,128)(2,1)S(1)}, bf16[512,1024]{1,0:T(8,128)(2,1)}, u32[]{:S(2)}) copy-start(bf16[512,1024]{1,0:T(8,128)(2,1)} %copy.95) | copy-start | bytes 3145732
  515.5 6.8 copy-start.32
  522.3 2.3 copy-start.42
  522.3 2.3 copy-start.43
  522.3 42.7 %copy-start.3 = (f32[512,1024]{1,0:T(8,128)S(1)}, f32[512,1024]{1,0:T(8,128)}, u32[]{:S(2)}) copy-start(f32[512,1024]{1,0:T(8,128)} %copy-done.2) | copy-start | bytes 6291460
  (13 other events, 15.4 us)
Sparse Core Ops, SparseCore 0:
  11.0 72.4 all-gather.8
  97.8 27.9 all-gather.16
  128.7 55.9 all-gather.10
  187.6 76.1 all-gather.12
  266.6 75.9 all-gather.14
  369.1 27.6 all-gather.18
  399.7 141.8 reduce-scatter.6
  548.2 152.3 reduce-scatter.4
  703.5 185.7 reduce-scatter.8
  892.1 184.3 reduce-scatter.10
where the time goes:
time: 1090 us; the launch traced here: 1080 us
  waiting for transfers between devices  683 us (63%)
  matrix products  146 us (13%)
  blocking collectives  125 us (11%)
  local copies, waits for them, and re-layouts  51.6 us (5%)
  other arithmetic  50 us (5%)
  between operations  16.5 us (2%)
  loops' own time  11.1 us (1%)
    reduce_scatter x1, waiting for transfers between devices, on_device(): lax.psum_scatter(grad_up, ('dp', 'seq'), scatter_dimension=0, tiled=True)  189 us
    reduce_scatter x1, waiting for transfers between devices, on_device(): lax.psum_scatter(grad_down, ('dp', 'seq'), scatter_dimension=0, tiled=True)  187 us
    reduce_scatter x1, waiting for transfers between devices, on_device(): lax.psum_scatter(grad_in_weight, ('dp', 'seq'), scatter_dimension=0, tile...  131 us
    unnamed x3, blocking collectives  96.3 us
    all_gather x1, waiting for transfers between devices, on_device(): lax.all_gather(up_projection_weight, ('dp', 'seq'), axis=0, tiled=True)  74 us
    all_gather x1, waiting for transfers between devices, on_device(): lax.all_gather(down_projection_weight, ('dp', 'seq'), axis=0, tiled=True)  67 us
    dot_general x4, matrix products, rows_product(): lax.dot_general(factor_one, factor_two, (((0,), (0,)), ((), ())), preferr...  36.1 us
    all_gather x2, blocking collectives, prefix(): lax.all_gather(part.astype(kind), axis)  28.2 us
  transfers between devices with their start and end apart: 10, of which 7 were waited for; matrix products, arithmetic and copies ran while one was open for 18% of the time, Pallas kernels for 0%

commit v1 on v0

--- a/solution.py
+++ b/solution.py
@@ -1,6 +1,8 @@
 import jax
 import jax.numpy as jnp
 from jax import lax
+from jax.experimental import pallas as pl
+from jax.experimental.pallas import tpu as pltpu
 from jax.sharding import PartitionSpec as P
 
 HEAD = 64
@@ -62,7 +64,7 @@
     )
 
 
-def on_device(
+def on_device_general(
     tokens,
     starts,
     query_key_value_weight,
@@ -322,9 +324,577 @@
     )
 
 
+MESH = pl.DeviceIdType.MESH
+LOW = jnp.bfloat16
+FULL = jnp.float32
+
+
+class Place:
+    def __init__(self):
+        dp, seq = lax.axis_index("dp"), lax.axis_index("seq")
+        self.y, self.x = dp // 2, dp % 2
+        self.z, self.c = seq // 2, seq % 2
+        self.dp, self.seq = dp, seq
+        self.over_x = (self.y * 2 + 1 - self.x, seq)
+        self.over_y = ((1 - self.y) * 2 + self.x, seq)
+        self.sibling = (dp, self.z * 2 + 1 - self.c)
+        self.along_z = [(dp, (self.z + d) % 4 * 2 + self.c) for d in (1, 2, 3)]
+
+    def meet(self):
+        barrier = pltpu.get_barrier_semaphore()
+        everyone = [self.over_x, self.over_y, self.sibling, *self.along_z]
+        for device in everyone:
+            pl.semaphore_signal(barrier, inc=1, device_id=device, device_id_type=MESH)
+        pl.semaphore_wait(barrier, len(everyone))
+
+
+def remote(source, target, send, recv, device):
+    return pltpu.make_async_remote_copy(
+        src_ref=source,
+        dst_ref=target,
+        send_sem=send,
+        recv_sem=recv,
+        device_id=device,
+        device_id_type=MESH,
+    )
+
+
+class Gather:
+    def __init__(self, place, full, send, recv):
+        p = place
+        half = full.shape[4] // 2
+        low, high = pl.ds(0, half), pl.ds(half, half)
+        own = full.at[p.y, p.x, p.z, p.c]
+        parts = [(own, device) for device in p.along_z]
+        parts.append((full.at[p.y, p.x, :, p.c, low], p.over_x))
+        parts.append((full.at[p.y, p.x, :, p.c, high], p.over_y))
+        parts.append((full.at[p.y, :, :, p.c, low], p.over_y))
+        parts.append((full.at[:, p.x, :, p.c, high], p.over_x))
+        for y, x in ((p.y, p.x), (p.y, 1 - p.x), (1 - p.y, p.x), (1 - p.y, 1 - p.x)):
+            parts.append((full.at[y, x, :, p.c], p.sibling))
+        self.copies = [
+            remote(ref, ref, send.at[i], recv.at[i], device)
+            for i, (ref, device) in enumerate(parts)
+        ]
+
+    def start(self, *which):
+        for i in which:
+            self.copies[i].start()
+
+    def arrive(self, *which):
+        for i in which:
+            self.copies[i].wait_recv()
+
+    def step(self, number):
+        if number == 0:
+            self.start(0, 1, 2)
+        elif number == 1:
+            self.arrive(0, 1, 2)
+            self.start(3, 4, 7)
+        elif number == 2:
+            self.arrive(3, 4)
+            self.start(5, 6)
+        elif number == 3:
+            self.arrive(5, 6)
+            self.start(8, 9, 10)
+        else:
+            self.arrive(7, 8, 9, 10)
+
+    def finish(self):
+        for copy in self.copies:
+            copy.wait_send()
+
+
+class Scatter:
+    def __init__(self, place, own, total, pair, first_a, first_b, second_a, second_b, last, send, recv):
+        p = place
+        half = own.shape[4] // 2
+        self.place, self.half = p, half
+        self.own, self.total, self.pair = own, total, pair
+        self.first_a, self.first_b = first_a, first_b
+        self.second_a, self.second_b = second_a, second_b
+        self.last = last
+        low, high = pl.ds(0, half), pl.ds(half, half)
+        parts = [
+            (own.at[:, :, :, 1 - p.c], pair, p.sibling),
+            (total.at[1 - p.y, :, :, low], first_a, p.over_y),
+            (total.at[:, 1 - p.x, :, high], first_b, p.over_x),
+            (total.at[p.y, 1 - p.x, :, low], second_a, p.over_x),
+            (total.at[1 - p.y, p.x, :, high], second_b, p.over_y),
+        ]
+        self.keep = pltpu.make_async_copy(own.at[:, :, :, p.c], total, send.at[8])
+        for d in (1, 2, 3):
+            parts.append((total.at[p.y, p.x, (p.z + d) % 4], last.at[d - 1], p.along_z[d - 1]))
+        self.copies = [
+            remote(source, target, send.at[i], recv.at[i], device)
+            for i, (source, target, device) in enumerate(parts)
+        ]
+
+    def step(self, number):
+        p, half = self.place, self.half
+        low, high = slice(0, half), slice(half, 2 * half)
+        total = self.total
+        if number == 0:
+            self.copies[0].start()
+            self.keep.start()
+        elif number == 1:
+            self.keep.wait()
+            self.copies[0].wait_recv()
+
+            @pl.loop(0, 4)
+            def _(i):
+                y, x = i // 2, i % 2
+                total[y, x] = total[y, x] + self.pair[y, x]
+
+            self.copies[1].start()
+            self.copies[2].start()
+        elif number == 2:
+            self.copies[1].wait_recv()
+            self.copies[2].wait_recv()
+            for i in range(2):
+                total[p.y, i, :, low] += self.first_a[i]
+                total[i, p.x, :, high] += self.first_b[i]
+            self.copies[3].start()
+            self.copies[4].start()
+        elif number == 3:
+            self.copies[3].wait_recv()
+            self.copies[4].wait_recv()
+            total[p.y, p.x, :, low] += self.second_a[...]
+            total[p.y, p.x, :, high] += self.second_b[...]
+            for i in (5, 6, 7):
+                self.copies[i].start()
+
+    def result(self):
+        for i in (5, 6, 7):
+            self.copies[i].wait_recv()
+        p = self.place
+        value = total = self.total[p.y, p.x, p.z].astype(FULL)
+        for d in range(3):
+            value = value + self.last[d].astype(FULL)
+        return value
+
+    def finish(self):
+        for copy in self.copies:
+            copy.wait_send()
+
+
+def gather_kernel(inputs, outputs, wide, tall, pack, send, recv, sends, recvs, local):
+    p = Place()
+    for j in range(8):
+        source = inputs[min(j // 3, 2) if j < 4 else 2] if j != 3 else inputs[1]
+        column = j if j < 3 else (0 if j == 3 else j - 4)
+        wide[j, p.y, p.x, p.z, p.c] = source[:, column * 1024 : column * 1024 + 1024]
+    for j in range(4):
+        tall[j, p.y, p.x, p.z, p.c] = inputs[3][:, 256 * j : 256 * j + 256]
+    pack[p.y, p.x, p.z, p.c] = inputs[4][...]
+    p.meet()
+    small = SmallGather(p, pack, sends, recvs)
+    chunks = [Gather(p, wide.at[j], send.at[j], recv.at[j]) for j in range(8)]
+    chunks += [Gather(p, tall.at[j], send.at[8 + j], recv.at[8 + j]) for j in range(4)]
+    outs = []
+    for j in range(8):
+        target = outputs[0] if j < 3 else (outputs[1] if j == 3 else outputs[2])
+        column = j if j < 3 else (0 if j == 3 else j - 4)
+        outs.append(
+            pltpu.make_async_copy(
+                wide.at[j], target.at[:, :, :, :, :, pl.ds(column * 1024, 1024)], local.at[j]
+            )
+        )
+    for j in range(4):
+        outs.append(
+            pltpu.make_async_copy(
+                tall.at[j], outputs[3].at[:, :, :, :, :, pl.ds(256 * j, 256)], local.at[8 + j]
+            )
+        )
+    for tick in range(12 + 4):
+        for number in range(5):
+            j = tick - number
+            if 0 <= j < 12:
+                chunks[j].step(number)
+                if number == 4:
+                    outs[j].start()
+        if tick < 5:
+            small.step(tick)
+    outputs[4][...] = pack[...]
+    small.finish()
+    for chunk in chunks:
+        chunk.finish()
+    for copy in outs:
+        copy.wait()
+
+
+def gather_all(in_weight, out_weight, up_weight, down_weight, pack):
+    block = lambda rows, columns: jax.ShapeDtypeStruct((2, 2, 4, 2, rows, columns), LOW)
+
+    def body(*refs):
+        gather_kernel(refs[:5], refs[5:10], *refs[10:])
+
+    return pl.pallas_call(
+        body,
+        out_shape=[block(32, 3072), block(32, 1024), block(32, 4096), block(128, 1024), block(16, 128)],
+        in_specs=[pl.BlockSpec(memory_space=pltpu.VMEM)] * 5,
+        out_specs=[pl.BlockSpec(memory_space=pl.ANY)] * 4 + [pl.BlockSpec(memory_space=pltpu.VMEM)],
+        scratch_shapes=[
+            pltpu.VMEM((8, 2, 2, 4, 2, 32, 1024), LOW),
+            pltpu.VMEM((4, 2, 2, 4, 2, 128, 256), LOW),
+            pltpu.VMEM((2, 2, 4, 2, 16, 128), LOW),
+            pltpu.SemaphoreType.DMA((12, 11)),
+            pltpu.SemaphoreType.DMA((12, 11)),
+            pltpu.SemaphoreType.DMA((9,)),
+            pltpu.SemaphoreType.DMA((9,)),
+            pltpu.SemaphoreType.DMA((12,)),
+        ],
+        compiler_params=pltpu.CompilerParams(
+            collective_id=0, has_side_effects=True, vmem_limit_bytes=60 << 20
+        ),
+        name="gather_weights",
+    )(in_weight, out_weight, up_weight, down_weight, pack)
+
+
+def scatter_kernel(inputs, outputs, wide, tall, send, recv):
+    p = Place()
+    p.meet()
+    order = [8, 9, 10, 11, 4, 5, 6, 7, 3, 0, 1, 2]
+    chunks = []
+    places = []
+    for j in range(12):
+        if j < 8:
+            source = 0 if j < 3 else (1 if j == 3 else 2)
+            column = j if j < 3 else (0 if j == 3 else j - 4)
+            columns = pl.ds(column * 1024, 1024)
+            own, buffers, at = inputs[source].at[:, :, :, :, :, columns], wide, j
+        else:
+            source, columns, buffers, at = 3, pl.ds((j - 8) * 256, 256), tall, j - 8
+            own = inputs[3].at[:, :, :, :, :, columns]
+        chunks.append(Scatter(p, own, *[ref.at[at] for ref in buffers], send.at[j], recv.at[j]))
+        places.append((source, columns))
+    for tick in range(12 + 4):
+        for number in range(5):
+            if 0 <= tick - number < 12:
+                j = order[tick - number]
+                if number < 4:
+                    chunks[j].step(number)
+                else:
+                    source, columns = places[j]
+                    outputs[source][:, columns] = chunks[j].result()
+    for chunk in chunks:
+        chunk.finish()
+
+
+def scatter_buffers(count, rows, columns):
+    half = rows // 2
+    shapes = [
+        (2, 2, 4, rows, columns),
+        (2, 2, 4, rows, columns),
+        (2, 4, half, columns),
+        (2, 4, half, columns),
+        (4, half, columns),
+        (4, half, columns),
+        (3, rows, columns),
+    ]
+    return [pltpu.VMEM((count, *shape), LOW) for shape in shapes]
+
+
+def scatter_all(*grads):
+    def body(*refs):
+        scatter_kernel(refs[:4], refs[4:8], refs[8:15], refs[15:22], *refs[22:])
+
+    return pl.pallas_call(
+        body,
+        out_shape=[
+            jax.ShapeDtypeStruct(shape, FULL)
+            for shape in ((32, 3072), (32, 1024), (32, 4096), (128, 1024))
+        ],
+        in_specs=[pl.BlockSpec(memory_space=pl.ANY)] * 4,
+        out_specs=[pl.BlockSpec(memory_space=pltpu.VMEM)] * 4,
+        scratch_shapes=scatter_buffers(8, 32, 1024)
+        + scatter_buffers(4, 128, 256)
+        + [pltpu.SemaphoreType.DMA((12, 9)), pltpu.SemaphoreType.DMA((12, 8))],
+        compiler_params=pltpu.CompilerParams(
+            collective_id=1, has_side_effects=True, vmem_limit_bytes=60 << 20
+        ),
+        name="scatter_gradients",
+    )(*[grad.reshape(2, 2, 4, 2, grad.shape[0] // 32, grad.shape[1]) for grad in grads])
+
+
+class SmallGather(Gather):
+    def __init__(self, place, full, send, recv):
+        p = place
+        own = full.at[p.y, p.x, p.z, p.c]
+        parts = [(own, device) for device in p.along_z]
+        parts.append((full.at[p.y, p.x, :, p.c], p.over_x))
+        parts.append((full.at[p.y, :, :, p.c], p.over_y))
+        for y in range(2):
+            for x in range(2):
+                parts.append((full.at[y, x, :, p.c], p.sibling))
+        self.copies = [
+            remote(ref, ref, send.at[i], recv.at[i], device)
+            for i, (ref, device) in enumerate(parts)
+        ]
+
+    def step(self, number):
+        if number == 0:
+            self.start(0, 1, 2)
+        elif number == 1:
+            self.arrive(0, 1, 2)
+            self.start(3)
+        elif number == 2:
+            self.arrive(3)
+            self.start(4)
+        elif number == 3:
+            self.arrive(4)
+            self.start(5, 6, 7, 8)
+        else:
+            self.arrive(5, 6, 7, 8)
+
+
+def on_device(
+    tokens,
+    starts,
+    query_key_value_weight,
+    attention_output_weight,
+    up_projection_weight,
+    down_projection_weight,
+    first_gain,
+    first_shift,
+    second_gain,
+    second_shift,
+    cotangent,
+):
+    local_len = tokens.shape[1]
+    model_width = tokens.shape[2]
+    head_count = model_width // HEAD
+    block_count = local_len // BLOCK
+    block_shape = (block_count, BLOCK, head_count, HEAD)
+    zero_low = jnp.zeros((), jnp.bfloat16)
+    input_tokens = tokens[0].astype(jnp.float32)
+    first_pos = lax.axis_index("seq") * local_len
+    positions = first_pos + jnp.arange(local_len, dtype=jnp.int32)
+    pack_starts = starts[0]
+    image_ids = jnp.sum((pack_starts[None, :] <= positions[:, None]).astype(jnp.int32), axis=1) - 1
+    before_id = jnp.sum((pack_starts <= first_pos - 1).astype(jnp.int32)) - 1
+    causal = jnp.arange(BLOCK)[:, None] >= jnp.arange(BLOCK)[None, :]
+    mine = lax.axis_index("dp") * 8 + lax.axis_index("seq")
+    pack = jnp.stack([first_gain, first_shift, second_gain, second_shift]).astype(FULL)
+    pack = jnp.roll(jnp.pad(pack, ((0, 12), (0, 96))), 32 * (mine % 4), axis=1).astype(LOW)
+    in_full, out_full, up_full, down_full, packs = gather_all(
+        query_key_value_weight,
+        attention_output_weight,
+        up_projection_weight,
+        down_projection_weight,
+        pack,
+    )
+    in_full, out_full = in_full.reshape(1024, 3072), out_full.reshape(1024, 1024)
+    up_full, down_full = up_full.reshape(1024, 4096), down_full.reshape(4096, 1024)
+    packs = jnp.sum(packs.reshape(8, 4, 16, 128).astype(FULL), axis=1)
+    packs = jnp.transpose(packs[:, :4], (1, 0, 2)).reshape(4, 1024)
+    gain_one, shift_one, gain_two, shift_two = packs[0], packs[1], packs[2], packs[3]
+    first_normed_tokens = layer_norm(input_tokens, gain_one, shift_one)
+    normed_low = first_normed_tokens.astype(jnp.bfloat16)
+    projected_tokens = jnp.dot(normed_low, in_full, preferred_element_type=jnp.float32)
+    queries = projected_tokens[:, :model_width]
+    keys_raw = projected_tokens[:, model_width : 2 * model_width]
+    values_raw = projected_tokens[:, 2 * model_width :]
+    feat_query = feature(queries).astype(jnp.bfloat16).reshape(block_shape)
+    feat_key = feature(keys_raw).astype(jnp.bfloat16).reshape(block_shape)
+    value_low = values_raw.astype(jnp.bfloat16).reshape(block_shape)
+    block_number = 0
+    last_id = image_ids[-1]
+    tail_mask = image_ids == last_id
+    tail_key = jnp.where(tail_mask[:, None, None], feat_key[block_number], zero_low)
+    keep_list = [image_ids == before_id]
+    tail_list = [tail_mask]
+    flag_list = [(last_id == before_id).astype(jnp.float32)]
+    same_list = [causal & (image_ids[:, None] == image_ids[None, :])]
+    update_list = [
+        jnp.einsum(
+            "jhe,jhf->hef", tail_key, value_low[block_number], preferred_element_type=jnp.float32
+        )
+    ]
+    total_list = [jnp.sum(tail_key.astype(jnp.float32), axis=0)]
+    identity = (
+        jnp.ones((), jnp.float32),
+        jnp.zeros((head_count, HEAD, HEAD), jnp.float32),
+        jnp.zeros((head_count, HEAD), jnp.float32),
+    )
+    combined = identity
+    block_number = 0
+    combined = combine(
+        combined, (flag_list[block_number], update_list[block_number], total_list[block_number])
+    )
+    entering = prefix(combined, "seq", combine, identity, False)
+    memory = entering[1]
+    key_sum = entering[2]
+    block_number = 0
+    query_block = feat_query[block_number]
+    keep_float = keep_list[block_number].astype(jnp.float32)
+    memory_low = memory.astype(jnp.bfloat16)
+    raw_scores = jnp.einsum(
+        "the,jhe->htj", query_block, feat_key[block_number], preferred_element_type=jnp.float32
+    )
+    masked = jnp.where(same_list[block_number][None], raw_scores, 0.0)
+    scores_low = masked.astype(jnp.bfloat16)
+    carried = (
+        jnp.einsum("the,hef->thf", query_block, memory_low, preferred_element_type=jnp.float32)
+        * keep_float[:, None, None]
+    )
+    numerator = (
+        jnp.einsum(
+            "htj,jhf->thf", scores_low, value_low[block_number], preferred_element_type=jnp.float32
+        )
+        + carried
+    )
+    denominator = jnp.transpose(jnp.sum(masked, axis=2)) + keep_float[:, None] * jnp.sum(
+        query_block.astype(jnp.float32) * key_sum[None], axis=2
+    )
+    memory_list = [memory_low]
+    keysum_list = [key_sum]
+    numer_list = [numerator]
+    denom_list = [denominator]
+    ratio_list = numerator / denominator[:, :, None]
+    mixed_low = ratio_list.reshape(local_len, model_width).astype(jnp.bfloat16)
+    middle_tokens = input_tokens + jnp.dot(mixed_low, out_full, preferred_element_type=jnp.float32)
+    normed_two_low = layer_norm(middle_tokens, gain_two, shift_two).astype(jnp.bfloat16)
+    upper_hidden = jnp.dot(normed_two_low, up_full, preferred_element_type=jnp.float32)
+    active_low = jax.nn.gelu(upper_hidden).astype(jnp.bfloat16)
+    result = middle_tokens + jnp.dot(active_low, down_full, preferred_element_type=jnp.float32)
+    result_tokens = result.astype(jnp.bfloat16).reshape(1, local_len, model_width)
+    grad_out = cotangent[0].astype(jnp.float32)
+    grad_out_low = cotangent[0]
+    grad_down = rows_product(active_low, grad_out_low)
+    d_active = cols_product(grad_out_low, down_full)
+    gelu_value, gelu_back = jax.vjp(jax.nn.gelu, upper_hidden)
+    g_upper = gelu_back(d_active)[0].astype(jnp.bfloat16)
+    grad_up = rows_product(normed_two_low, g_upper)
+    d_normed_two = cols_product(g_upper, up_full)
+    norm_value, norm_back = jax.vjp(layer_norm, middle_tokens, gain_two, shift_two)
+    middle_part, grad_gain_two, grad_shift_two = norm_back(d_normed_two)
+    g_middle = grad_out + middle_part
+    g_middle_low = g_middle.astype(jnp.bfloat16)
+    grad_out_weight = rows_product(mixed_low, g_middle_low)
+    d_mixed = cols_product(g_middle_low, out_full).reshape(block_shape)
+    block_number = 0
+    query_block = feat_query[block_number]
+    denominator = denom_list[block_number]
+    g_numerator = (d_mixed[block_number] / denominator[:, :, None]).astype(jnp.bfloat16)
+    g_denominator = -jnp.sum(d_mixed[block_number] * numer_list[block_number], axis=2) / (
+        denominator * denominator
+    )
+    kept_query = jnp.where(keep_list[block_number][:, None, None], query_block, zero_low)
+    gnum_list = [g_numerator]
+    gden_list = [g_denominator]
+    local_list = [
+        jnp.einsum("the,thf->hef", kept_query, g_numerator, preferred_element_type=jnp.float32)
+    ]
+    localkey_list = [jnp.sum(kept_query.astype(jnp.float32) * g_denominator[:, :, None], axis=0)]
+    combined = identity
+    for block_number in reversed(range(block_count)):
+        combined = combine(
+            combined,
+            (flag_list[block_number], local_list[block_number], localkey_list[block_number]),
+        )
+    leaving = prefix(combined, "seq", combine, identity, True)
+    g_memory = leaving[1]
+    g_key_sum = leaving[2]
+    gq_list = []
+    gk_list = []
+    gv_list = []
+    for block_number in reversed(range(block_count)):
+        query_block = feat_query[block_number]
+        key_block = feat_key[block_number]
+        value_block = value_low[block_number]
+        keep_float = keep_list[block_number].astype(jnp.float32)
+        tail_float = tail_list[block_number].astype(jnp.float32)
+        g_numerator = gnum_list[block_number]
+        g_denominator = gden_list[block_number]
+        g_update = g_memory.astype(jnp.bfloat16)
+        raw_scores = jnp.einsum(
+            "the,jhe->htj", query_block, key_block, preferred_element_type=jnp.float32
+        )
+        scores_low = jnp.where(same_list[block_number][None], raw_scores, 0.0).astype(jnp.bfloat16)
+        g_scores = (
+            jnp.einsum("thf,jhf->htj", g_numerator, value_block, preferred_element_type=jnp.float32)
+            + jnp.transpose(g_denominator)[:, :, None]
+        )
+        g_scores_low = jnp.where(
+            same_list[block_number][None], g_scores.astype(jnp.bfloat16), zero_low
+        )
+        query_grad = jnp.einsum(
+            "htj,jhe->the", g_scores_low, key_block, preferred_element_type=jnp.float32
+        )
+        query_grad = query_grad + keep_float[:, None, None] * (
+            jnp.einsum(
+                "thf,hef->the",
+                g_numerator,
+                memory_list[block_number],
+                preferred_element_type=jnp.float32,
+            )
+            + g_denominator[:, :, None] * keysum_list[block_number][None]
+        )
+        key_grad = jnp.einsum(
+            "htj,the->jhe", g_scores_low, query_block, preferred_element_type=jnp.float32
+        )
+        key_grad = key_grad + tail_float[:, None, None] * (
+            jnp.einsum("jhf,hef->jhe", value_block, g_update, preferred_element_type=jnp.float32)
+            + g_key_sum[None]
+        )
+        tail_key = jnp.where(tail_list[block_number][:, None, None], key_block, zero_low)
+        value_grad = jnp.einsum(
+            "htj,thf->jhf", scores_low, g_numerator, preferred_element_type=jnp.float32
+        )
+        value_grad = value_grad + jnp.einsum(
+            "jhe,hef->jhf", tail_key, g_update, preferred_element_type=jnp.float32
+        )
+        gq_list.append(query_grad)
+        gk_list.append(key_grad)
+        gv_list.append(value_grad)
+        g_memory = local_list[block_number] + flag_list[block_number] * g_memory
+        g_key_sum = localkey_list[block_number] + flag_list[block_number] * g_key_sum
+    d_feat_query = jnp.concatenate(gq_list[::-1], axis=0).reshape(local_len, model_width)
+    d_feat_key = jnp.concatenate(gk_list[::-1], axis=0).reshape(local_len, model_width)
+    d_value = jnp.concatenate(gv_list[::-1], axis=0).reshape(local_len, model_width)
+    query_value, query_back = jax.vjp(feature, queries)
+    key_value, key_back = jax.vjp(feature, keys_raw)
+    g_projected = jnp.concatenate(
+        [query_back(d_feat_query)[0], key_back(d_feat_key)[0], d_value], axis=1
+    ).astype(jnp.bfloat16)
+    grad_in_weight = rows_product(normed_low, g_projected)
+    d_normed = cols_product(g_projected, in_full)
+    first_value, first_back = jax.vjp(layer_norm, input_tokens, gain_one, shift_one)
+    input_part, grad_gain_one, grad_shift_one = first_back(d_normed)
+    grad_tokens = (g_middle + input_part).reshape(1, local_len, model_width)
+    weights = scatter_all(
+        grad_in_weight.astype(LOW),
+        grad_out_weight.astype(LOW),
+        grad_up.astype(LOW),
+        grad_down.astype(LOW),
+    )
+    summed = (
+        *weights,
+        lax.psum_scatter(grad_gain_one, ("dp", "seq"), scatter_dimension=0, tiled=True),
+        lax.psum_scatter(grad_shift_one, ("dp", "seq"), scatter_dimension=0, tiled=True),
+        lax.psum_scatter(grad_gain_two, ("dp", "seq"), scatter_dimension=0, tiled=True),
+        lax.psum_scatter(grad_shift_two, ("dp", "seq"), scatter_dimension=0, tiled=True),
+    )
+    return (
+        result_tokens,
+        grad_tokens,
+        summed[0],
+        summed[1],
+        summed[2],
+        summed[3],
+        summed[4],
+        summed[5],
+        summed[6],
+        summed[7],
+    )
+
+
 def solution(mesh):
+
+    fast = dict(mesh.shape) == {"dp": 4, "seq": 8}
     return jax.shard_map(
-        on_device,
+        on_device if fast else on_device_general,
         mesh=mesh,
         in_specs=(
             P("dp", "seq", None),

time: 1090 us -> 584 us (0.54)
  waiting for transfers between devices: 683 us -> 0.04 us
  Pallas kernels: 0 us -> 243 us
  blocking collectives: 125 us -> 88.3 us
  matrix products: 146 us -> 127 us
    reduce_scatter x4 -> x0, waiting for transfers between devices: 507 us -> none  [the longest x1 189 us: on_device(): lax.psum_scatter(grad_up, ('dp', 'seq'), scatter_dimension=0, tiled=True)]
    pallas_call x0 -> x2, Pallas kernels: none -> 243 us  [the longest x1 124 us: gather_all(): pl.pallas_call(body, out_shape=[block(32, 3072), block(32, 1024), block(3...]
    all_gather x4 -> x0, waiting for transfers between devices: 174 us -> none  [the longest x1 74 us: on_device(): lax.all_gather(up_projection_weight, ('dp', 'seq'), axis=0, tiled=True)]
    unnamed x3 -> x2, blocking collectives: 96.3 us -> 59.9 us
    unnamed x117 -> x53, local copies, waits for them, and re-layouts: 23.9 us -> 17.3 us
  transfers between devices with their start and end apart: 10 -> 2, of which waited for: 7 -> 0; matrix products, arithmetic and copies ran while one was open for 18% -> 9% of each run, Pallas kernels for 0% -> 0%
where the time goes in v1:
time: 584 us; the launch traced here: 576 us
  Pallas kernels  243 us (42%)
  matrix products  127 us (22%)
  blocking collectives  88.3 us (15%)
  other arithmetic  45.7 us (8%)
  local copies, waits for them, and re-layouts  45.1 us (8%)
  between operations  16.3 us (3%)
  loops' own time  11.1 us (2%)
    pallas_call x1, Pallas kernels, gather_all(): pl.pallas_call(body, out_shape=[block(32, 3072), block(32, 1024), block(3...  124 us
    pallas_call x1, Pallas kernels, scatter_all(): pl.pallas_call(body, out_shape=[jax.ShapeDtypeStruct(shape, FULL) for sha...  120 us
    unnamed x2, blocking collectives  59.9 us
    dot_general x4, matrix products, rows_product(): lax.dot_general(factor_one, factor_two, (((0,), (0,)), ((), ())), preferr...  29.4 us
    dot_general x4, matrix products, cols_product(): lax.dot_general(factor_one, factor_two, (((1,), (1,)), ((), ())), preferr...  28.5 us
    all_gather x2, blocking collectives, prefix(): lax.all_gather(part.astype(kind), axis)  28.3 us
    select_n x32, other arithmetic, lap(): return jax.tree.map(lambda a, b: jnp.where(reached, a, b), new, before)  20.7 us
    unnamed x53, local copies, waits for them, and re-layouts  17.3 us
  transfers between devices with their start and end apart: 2, of which 0 were waited for; matrix products, arithmetic and copies ran while one was open for 9% of the time, Pallas kernels for 0%

profile of v1, /device:TPU:0, one launch (start us, length us, event | category | flops | bytes accessed | tf_op | source)
XLA Modules:
  0.0 576.5 jit_solution(4974352378149064486)
XLA Ops:
  9.5 123.6 %gather_weights.1 = (bf16[2,2,4,2,32,3072]{5,4,3,2,1,0:T(8,128)(2,1)}, bf16[2,2,4,2,32,1024]{5,4,3,2,1,0:T(8,128)(2,1)}, bf16[2,2,4,2,32,4096]{5,4,3,2,1,0:T(8,1...) custom-call(bf16[32,3072]{1,0:T(8,128)(2,1)} %refs_0_.1, bf16[32,1024]{1,0:T(8,128)(2,1)} %refs_1_.1, ...), custom_call_target="tpu_custom_call" | custom-call | tf_op jit(solution)/shard_map/gather_weights/pallas_call | solution.py:532
  137.4 5.8 fusion.51
  143.1 2.6 copy-done.1
  145.7 2.1 select_reduce_fusion.1
  148.4 1.9 copy.79
  153.5 20.6 %all-reduce.1 = bf16[8]{0:T(256)(128)(2,1)S(1)} all-reduce(bf16[8]{0:T(256)(128)(2,1)S(1)} %dynamic-update-slice), channel_id=1, replica_groups=mesh['dp'=4,'seq'=8] {'seq'}, use_global_device_ids=true, to_apply=%add.1 | all-reduce | flops 8 | bytes 32
  174.2 3.5 fusion.46
  177.6 2.3 copy.80
  180.0 14.2 %all_gather.32 = bf16[8,16,64]{2,1,0:T(8,128)(2,1)S(1)} all-gather(bf16[1,16,64]{2,1,0:T(8,128)(2,1)S(1)} %convert_element_type.240), channel_id=1, replica_groups=mesh['dp'=4,'seq'=8] {'seq'}, dimensions={0}, use_global_device_ids=true | all-gather | bytes 18432 | tf_op jit(solution)/shard_map/all_gather | solution.py:15
  194.4 4.0 select_reduce_fusion
  198.5 3.2 copy-done.20
  201.7 3.0 fusion.19
  204.6 20.5 %while.34 = (s32[]{:T(128)}, f32[16,64,64]{2,1,0:T(8,128)S(1)}, f32[16,64]{1,0:T(8,128)S(1)}, s32[]{:T(128)}, bf16[8]{0:T(256)(128)(2,1)S(1)}, /*index=5*/bf16[8...) while((s32[]{:T(128)}, f32[16,64,64]{2,1,0:T(8,128)S(1)}, ...), condition=%wide.region_8.9_spmd.clone, body=%wide.region_7.8_spmd.clone.sunk | while | flops 332805 | bytes 665753 | solution.py:33
  225.2 1.6 multiply_reduce_fusion.4
  226.9 2.6 fusion.39
  229.5 1.4 fusion.115
  231.2 10.3 %fusion.108 = f32[512,4096]{1,0:T(8,128)} fusion(bf16[1024,4096]{1,0:T(8,128)(2,1)} %bitcast.233, f32[512,1024]{1,0:T(8,128)S(1)} %get-tuple-element.445, f32[1024]{0:T(1024)S(1)} %bitcast.226, f32[1024]{0:T(1024)S(1)} %bitcast.220, f32[512]{0:T(512)S(1)} %fusion.96, f32[512]{0:T(512)S(1)} %broadcast_multiply_fusion), kind=kOutput, calls=%fused_computation.179 | convolution fusion | flops 4297588736 | bytes 18886656 | tf_op jit(solution)/shard_map/dot_general | solution.py:758
  241.5 12.0 %fusion.47 = bf16[1,512,1024]{2,1,0:T(8,128)(2,1)} fusion(f32[512,1024]{1,0:T(8,128)S(1)} %get-tuple-element.445, bf16[4096,1024]{1,0:T(8,128)(2,1)} %bitcast.235, f32[512,4096]{1,0:T(8,128)} %fusion.108), kind=kOutput, calls=%fused_computation.93 | convolution fusion | flops 4314890240 | bytes 19922944 | tf_op jit(solution)/shard_map/dot_general | solution.py:760
  253.5 12.8 %fusion.10 = bf16[512,4096]{1,0:T(8,128)(2,1)S(1)} fusion(f32[512,4096]{1,0:T(8,128)} %fusion.108, bf16[4096,1024]{1,0:T(8,128)(2,1)} %bitcast.236, bf16[1,512,1024]{2,1,0:T(8,128)(2,1)S(1)} %copy-done.8), kind=kOutput, calls=%fused_computation.19 | convolution fusion | flops 4336910336 | bytes 22020096 | tf_op jit(solution)/shard_map/dot_general | solution.py:62
  266.3 7.9 %multiply_reduce_fusion = (f32[1024]{0:T(1024)S(1)}, f32[512]{0:T(512)S(1)}, f32[1024]{0:T(1024)S(1)}, f32[512,1024]{1,0:T(8,128)S(1)}) fusion(f32[512,1024]{1,0:T(8,128)S(1)} %get-tuple-element.445, f32[512]{0:T(512)S(1)} %fusion.96, f32[512]{0:T(512)S(1)} %broadcast_multiply_fusion, f32[1024]{0:T(1024)S(1)} %bitcast.221, ...), kind=kOutput, calls=%fused_computation.67 | convolution fusion | flops 4299159040 | bytes 16795648 | tf_op jit(solution)/shard_map/dot_general | solution.py:62
  276.3 1.3 fusion.40
  277.7 7.8 %fusion.18 = f32[16,64,512]{2,1,0:T(8,128)} fusion(bf16[512,16,64]{0,2,1:T(8,128)(2,1)S(1)} %get-tuple-element.433, bf16[16,512,512]{1,2,0:T(8,128)(2,1)} %copy-done.20, pred[512,512]{0,1:T(8,128)(4,1)S(1)} %fusion.68), kind=kOutput, calls=%fused_computation.40 | convolution fusion | flops 541065216 | bytes 11796480 | tf_op jit(solution)/shard_map/htj,thf->jhf/dot_general | solution.py:842
  285.4 1.8 fusion.77
  287.3 2.6 convolution_convert_fusion.3
  289.9 7.4 %convolution_convert_fusion.1 = bf16[1024,4096]{1,0:T(8,128)(2,1)} fusion(bf16[512,4096]{1,0:T(8,128)(2,1)S(1)} %fusion.10, f32[512,1024]{1,0:T(8,128)S(1)} %get-tuple-element.445, f32[1024]{0:T(1024)S(1)} %bitcast.227, f32[1024]{0:T(1024)S(1)} %bitcast.223, f32[512]{0:T(512)S(1)} %fusion.96, f32[512]{0:T(512)S(1)} %broadcast_multiply_fusion), kind=kOutput, calls=%fused_computation.28 | convolution fusion | flops 4301783040 | bytes 14692352 | tf_op jit(solution)/shard_map/dot_general | solution.py:56
  298.5 1.6 mul.389
  300.1 3.0 copy.90
  303.0 3.5 multiply_reduce_fusion.1
  306.7 14.1 %all_gather.35 = bf16[8,16,64]{2,1,0:T(8,128)(2,1)S(1)} all-gather(bf16[1,16,64]{2,1,0:T(8,128)(2,1)S(1)} %convert_element_type.258), channel_id=1, replica_groups=mesh['dp'=4,'seq'=8] {'seq'}, dimensions={0}, use_global_device_ids=true | all-gather | bytes 18432 | tf_op jit(solution)/shard_map/all_gather | solution.py:15
  320.8 3.7 add_convert_fusion
  324.5 4.0 fusion.14
  328.6 3.3 fusion.38
  331.9 3.1 copy.87
  335.0 12.8 %convolution_convert_fusion = bf16[4096,1024]{1,0:T(8,128)(2,1)} fusion(bf16[1,512,1024]{2,1,0:T(8,128)(2,1)} %param.25, f32[512,4096]{1,0:T(8,128)} %fusion.108), kind=kOutput, calls=%fused_computation.27 | convolution fusion | flops 4318035968 | bytes 17825792 | tf_op jit(solution)/shard_map/dot_general | solution.py:56
  347.8 20.6 %while.35 = (s32[]{:T(128)}, f32[16,64,64]{2,1,0:T(8,128)S(1)}, f32[16,64]{1,0:T(8,128)S(1)}, s32[]{:T(128)}, bf16[8]{0:T(256)(128)(2,1)S(1)}, /*index=5*/bf16[8...) while((s32[]{:T(128)}, f32[16,64,64]{2,1,0:T(8,128)S(1)}, ...), condition=%wide.region_18.19_spmd.clone, body=%wide.region_17.18_spmd.clone.sunk | while | flops 332809 | bytes 665815 | solution.py:33
  368.4 3.4 add_convert_fusion.1
  371.8 2.3 copy.95
  374.1 3.3 multiply_add_fusion
  377.4 3.0 copy.91
  380.4 4.2 add_convert_fusion.3
  384.7 6.4 %fusion.109 = (f32[1024]{0:T(1024)S(1)}, f32[512]{0:T(512)S(1)}, f32[512,1024]{1,0:T(8,128)S(1)}) fusion(f32[1024]{0:T(1024)S(1)} %bitcast.216, f32[512]{0:T(512)S(1)} %broadcast_multiply_fusion.1, bf16[1,512,1024]{2,1,0:T(8,128)(2,1)S(1)} %copy-done, bf16[1024,3072]{1,0:T(8,128)(2,1)} %bitcast.238, bf16[512,1024]{1,0:T(8,128)(2,1)S(1)} %copy-done.14, ...), kind=kOutput, calls=%fused_computation.180 | convolution fusion | flops 3233806848 | bytes 12595200 | tf_op jit(solution)/shard_map/dot_general | solution.py:62
  391.1 6.5 %convolution_convert_fusion.2 = bf16[1024,3072]{1,0:T(8,128)(2,1)} fusion(bf16[512,1024]{1,0:T(8,128)(2,1)S(1)} %copy-done.14, bf16[512,1024]{1,0:T(8,128)(2,1)S(1)} %get-tuple-element.430, bf16[512,1024]{1,0:T(8,128)(2,1)S(1)} %get-tuple-element.429, bf16[1,512,1024]{2,1,0:T(8,128)(2,1)S(1)} %copy-done, f32[1024]{0:T(1024)S(1)} %bitcast.225, ...), kind=kOutput, calls=%fused_computation.31 | convolution fusion | flops 3236954112 | bytes 10498048 | tf_op jit(solution)/shard_map/dot_general | solution.py:56
  399.5 2.2 add_bitcast_fusion
  401.7 119.8 %scatter_gradients.1 = (f32[32,3072]{1,0:T(8,128)}, f32[32,1024]{1,0:T(8,128)}, f32[32,4096]{1,0:T(8,128)}, f32[128,1024]{1,0:T(8,128)}) custom-call(bf16[2,2,4,2,32,3072]{5,4,3,2,1,0:T(8,128)(2,1)} %bitcast.196, bf16[2,2,4,2,32,1024]{5,4,3,2,1,0:T(8,128)(2,1)} %bitcast.206, bf16[2,2,4,2,32,4096]{5,4,3,2,1,0:T(8,128)(2,1)} %bitcast.192, ...), custom_call_target="tpu_custom_call" | custom-call | tf_op jit(solution)/shard_map/scatter_gradients/pallas_call | solution.py:602
  521.6 39.3 %all-reduce.6 = (f32[1024]{0:T(1024)S(1)}, f32[1024]{0:T(1024)S(1)}, f32[1024]{0:T(1024)S(1)}, f32[1024]{0:T(1024)S(1)}) all-reduce(f32[1024]{0:T(1024)S(1)} %get-tuple-element.384, f32[1024]{0:T(1024)S(1)} %get-tuple-element.387, f32[1024]{0:T(1024)S(1)} %get-tuple-element.382, ...), channel_id=4, replica_groups=mesh['dp'=4,'seq'=8] {'dp','seq'}, use_global_device_ids=true, to_apply=%region_22.23.clone | all-reduce | flops 4096 | bytes 32768
  563.2 1.8 copy.127
  565.0 1.6 copy.128
  566.5 1.9 copy.129
  (141 shorter events, 47.9 us)
Async XLA Ops:
  7.2 127.6 %copy-start.18 = (s32[1,13]{1,0:T(1,128)S(1)}, s32[1,13]{1,0:T(1,128)}, u32[]{:S(2)}) copy-start(s32[1,13]{1,0:T(1,128)} %param.16) | copy-start | bytes 160
  7.2 127.0 %copy-start = (bf16[1,512,1024]{2,1,0:T(8,128)(2,1)S(1)}, bf16[1,512,1024]{2,1,0:T(8,128)(2,1)}, u32[]{:S(2)}) copy-start(bf16[1,512,1024]{2,1,0:T(8,128)(2,1)} %param.15) | copy-start | bytes 3145732
  7.2 197.4 %all-gather.5.cloned.1.call-start = ((), (), s32[]{:S(2)}) async-start(), calls=%async_computation | async-start | bytes 2359296 | tf_op jit(solution)/shard_map/all_gather | solution.py:15
  134.8 8.3 %copy-start.16 = (f32[512]{0:T(512)}, f32[512]{0:T(512)S(1)}, u32[]{:S(2)}) copy-start(f32[512]{0:T(512)S(1)} %fusion.31) | copy-start | bytes 6148
  143.1 2.6 copy-start.1
  148.4 3.0 copy-start.6
  150.3 1.9 copy-start.19
  151.4 196.4 %all-gather.7.cloned.1.call-start = ((), (), s32[]{:S(2)}) async-start(), calls=%async_computation.1 | async-start | bytes 2359296 | tf_op jit(solution)/shard_map/all_gather | solution.py:15
  198.4 3.2 copy-start.20
  226.9 2.6 copy-start.13
  241.5 12.0 %copy-start.8 = (bf16[1,512,1024]{2,1,0:T(8,128)(2,1)S(1)}, bf16[1,512,1024]{2,1,0:T(8,128)(2,1)}, u32[]{:S(2)}) copy-start(bf16[1,512,1024]{2,1,0:T(8,128)(2,1)} %param.25) | copy-start | bytes 3145732
  275.0 1.3 copy-start.2
  277.7 19.7 %copy-start.5 = (bf16[512,16,64]{0,2,1:T(8,128)(2,1)}, bf16[512,16,64]{0,2,1:T(8,128)(2,1)S(1)}, u32[]{:S(2)}) copy-start(bf16[512,16,64]{0,2,1:T(8,128)(2,1)S(1)} %get-tuple-element.433) | copy-start | bytes 3145732
  289.9 7.4 %copy-start.10 = (bf16[512,1024]{0,1:T(8,128)(2,1)S(1)}, bf16[512,1024]{0,1:T(8,128)(2,1)}, u32[]{:S(2)}) copy-start(bf16[512,1024]{0,1:T(8,128)(2,1)} %copy.80) | copy-start | bytes 3145732
  320.8 3.7 copy-start.11
  324.5 4.0 copy-start.7
  324.5 4.0 copy-start.12
  377.4 3.0 copy-start.4
  380.4 4.2 copy-start.14
  391.1 6.5 %copy-start.17 = (f32[512]{0:T(512)S(1)}, f32[512]{0:T(512)}, u32[]{:S(2)}) copy-start(f32[512]{0:T(512)} %copy-done.16) | copy-start | bytes 6148
  397.7 1.6 copy-start.3
  397.7 1.9 copy-start.9
  521.6 46.9 %copy-start.15 = (f32[128,1024]{1,0:T(8,128)S(1)}, f32[128,1024]{1,0:T(8,128)}, u32[]{:S(2)}) copy-start(f32[128,1024]{1,0:T(8,128)} %get-tuple-element.611) | copy-start | bytes 1572868
Sparse Core Ops, SparseCore 0:
  151.5 33.1 all-gather.4
  298.6 26.9 all-gather.6

commit v2 on v1

--- a/solution.py
+++ b/solution.py
@@ -1,3 +1,5 @@
+import functools
+
 import jax
 import jax.numpy as jnp
 from jax import lax
@@ -338,11 +340,14 @@
         self.over_x = (self.y * 2 + 1 - self.x, seq)
         self.over_y = ((1 - self.y) * 2 + self.x, seq)
         self.sibling = (dp, self.z * 2 + 1 - self.c)
+        self.following = [(dp, (seq + 1) % 8), (dp, (seq + 2) % 8)]
+        self.preceding = [(dp, (seq + 7) % 8), (dp, (seq + 6) % 8)]
+        self.over_end = (dp, (seq + 2 * self.c + 7) % 8)
         self.along_z = [(dp, (self.z + d) % 4 * 2 + self.c) for d in (1, 2, 3)]
 
     def meet(self):
         barrier = pltpu.get_barrier_semaphore()
-        everyone = [self.over_x, self.over_y, self.sibling, *self.along_z]
+        everyone = [self.over_x, self.over_y, self.sibling, self.over_end, *self.along_z]
         for device in everyone:
             pl.semaphore_signal(barrier, inc=1, device_id=device, device_id_type=MESH)
         pl.semaphore_wait(barrier, len(everyone))
@@ -478,77 +483,496 @@
             copy.wait_send()
 
 
-def gather_kernel(inputs, outputs, wide, tall, pack, send, recv, sends, recvs, local):
+class SmallGather(Gather):
+    def __init__(self, place, full, send, recv):
+        p = place
+        own = full.at[p.y, p.x, p.z, p.c]
+        parts = [(own, device) for device in p.along_z]
+        parts.append((full.at[p.y, p.x, :, p.c], p.over_x))
+        parts.append((full.at[p.y, :, :, p.c], p.over_y))
+        for y in range(2):
+            for x in range(2):
+                parts.append((full.at[y, x, :, p.c], p.sibling))
+        self.copies = [
+            remote(ref, ref, send.at[i], recv.at[i], device)
+            for i, (ref, device) in enumerate(parts)
+        ]
+
+    def step(self, number):
+        if number == 0:
+            self.start(0, 1, 2)
+        elif number == 1:
+            self.arrive(0, 1, 2)
+            self.start(3)
+        elif number == 2:
+            self.arrive(3)
+            self.start(4)
+        elif number == 3:
+            self.arrive(4)
+            self.start(5, 6, 7, 8)
+        else:
+            self.arrive(5, 6, 7, 8)
+
+
+def product(one, two):
+    return jnp.dot(one, two, preferred_element_type=FULL)
+
+
+def across(one, two):
+    return lax.dot_general(one, two, (((1,), (1,)), ((), ())), preferred_element_type=FULL)
+
+
+def down_rows(one, two):
+    return lax.dot_general(one, two, (((0,), (0,)), ((), ())), preferred_element_type=FULL)
+
+
+def tile(i, size):
+    return pl.ds(pl.multiple_of(i * size, size), size)
+
+
+def image_count(starts, at):
+    total = jnp.where(starts[0, 0] <= at, 1, 0)
+    for k in range(1, starts.shape[1]):
+        total = total + jnp.where(starts[0, k] <= at, 1, 0)
+    return total
+
+
+class Images:
+    def __init__(self, starts, seq, length):
+        first = seq * length
+        self.length = length
+        self.column = image_count(starts, first + lax.broadcasted_iota(jnp.int32, (length, 128), 0))
+        self.row = image_count(starts, first + lax.broadcasted_iota(jnp.int32, (8, length), 1))
+        before = image_count(starts, first - 1)
+        last = image_count(starts, first + length - 1)
+        earlier = image_count(starts, first - length - 1)
+        later = image_count(starts, first + 2 * length - 1)
+        self.keep = jnp.where(self.column == before, 1.0, 0.0)
+        self.tail = jnp.where(self.column == last, 1.0, 0.0)
+        self.flag_before = jnp.where(before == earlier, 1.0, 0.0)
+        self.flag_after = jnp.where(later == last, 1.0, 0.0)
+
+
+def same_mask(images, rows, columns, transposed):
+    shape = (images.length, images.length)
+    down = lax.broadcasted_iota(jnp.int32, shape, 0)
+    along = lax.broadcasted_iota(jnp.int32, shape, 1)
+    order = down <= along if transposed else down >= along
+    equal = images.column[:, :1] == images.row[:1, :]
+    return jnp.where(order & equal, 1.0, 0.0).astype(LOW)
+
+
+def head_lanes(rows):
+    return lax.broadcasted_iota(jnp.int32, (rows, 128), 1) < HEAD
+
+
+def own_block():
+    return jnp.where(
+        (lax.broadcasted_iota(jnp.int32, (128, 128), 0) < HEAD)
+        == (lax.broadcasted_iota(jnp.int32, (128, 128), 1) < HEAD),
+        1.0,
+        0.0,
+    ).astype(LOW)
+
+
+def pack_pair(square):
+    return jnp.where(head_lanes(HEAD), square[:HEAD], square[HEAD:])
+
+
+def unpack_pair(packed):
+    lanes = head_lanes(HEAD)
+    zero = jnp.zeros_like(packed)
+    return jnp.concatenate([jnp.where(lanes, packed, zero), jnp.where(lanes, zero, packed)], axis=0)
+
+
+def statistics(values):
+    average = jnp.mean(values, axis=-1, keepdims=True)
+    centred = values - average
+    spread = jnp.mean(centred * centred, axis=-1, keepdims=True)
+    scale = lax.rsqrt(spread + 1e-05)
+    return centred * scale, scale
+
+
+def gelu_both(values):
+    root = 0.7978845608028654
+    square = values * values
+    angle = jnp.tanh(root * values * (1.0 + 0.044715 * square))
+    half = 0.5 + 0.5 * angle
+    slope = half + 0.5 * values * (1.0 - angle * angle) * (root * (1.0 + 0.134145 * square))
+    return values * half, slope
+
+
+def forward_kernel(inputs, outputs, scratch):
+    tokens_in, cotangent_in, starts, in_weight, out_weight, up_weight, down_weight, pack_in = inputs
+    (
+        in_full,
+        out_full,
+        up_full,
+        down_full,
+        grad_down_out,
+        result_out,
+        heads_out,
+        mixed_out,
+        inverse_out,
+        middle_out,
+        slope_out,
+        memory_out,
+        sums_out,
+        gains_out,
+    ) = outputs
+    (
+        wide,
+        tall,
+        pack,
+        tokens,
+        cotangent,
+        gains,
+        normed,
+        heads,
+        mask,
+        mixed,
+        mixed_low,
+        inverse,
+        middle,
+        active,
+        slope,
+        grad_down,
+        result,
+        outgoing,
+        incoming,
+        memory,
+        sums,
+        send,
+        recv,
+        small_send,
+        small_recv,
+        state_send,
+        state_recv,
+        local,
+        store,
+    ) = scratch
     p = Place()
+    length, width = tokens.shape
+    loads = []
     for j in range(8):
-        source = inputs[min(j // 3, 2) if j < 4 else 2] if j != 3 else inputs[1]
+        source = in_weight if j < 3 else (out_weight if j == 3 else up_weight)
         column = j if j < 3 else (0 if j == 3 else j - 4)
-        wide[j, p.y, p.x, p.z, p.c] = source[:, column * 1024 : column * 1024 + 1024]
+        loads.append((source.at[:, pl.ds(column * 1024, 1024)], wide.at[j, p.y, p.x, p.z, p.c]))
     for j in range(4):
-        tall[j, p.y, p.x, p.z, p.c] = inputs[3][:, 256 * j : 256 * j + 256]
-    pack[p.y, p.x, p.z, p.c] = inputs[4][...]
+        loads.append((down_weight.at[:, pl.ds(256 * j, 256)], tall.at[j, p.y, p.x, p.z, p.c]))
+    loads.append((pack_in, pack.at[p.y, p.x, p.z, p.c]))
+    loads.append((tokens_in, tokens))
+    loads.append((cotangent_in, cotangent))
+    loads = [pltpu.make_async_copy(a, b, local.at[i]) for i, (a, b) in enumerate(loads)]
+    for i in (12, 0, 1, 2, 13, 3, 4, 5, 6, 7, 8, 9, 10, 11, 14):
+        loads[i].start()
+    stores = []
+
+    def save(source, target):
+        copy = pltpu.make_async_copy(source, target, store.at[len(stores)])
+        copy.start()
+        stores.append(copy)
+
     p.meet()
-    small = SmallGather(p, pack, sends, recvs)
+    small = SmallGather(p, pack, small_send, small_recv)
     chunks = [Gather(p, wide.at[j], send.at[j], recv.at[j]) for j in range(8)]
     chunks += [Gather(p, tall.at[j], send.at[8 + j], recv.at[8 + j]) for j in range(4)]
-    outs = []
-    for j in range(8):
-        target = outputs[0] if j < 3 else (outputs[1] if j == 3 else outputs[2])
-        column = j if j < 3 else (0 if j == 3 else j - 4)
-        outs.append(
-            pltpu.make_async_copy(
-                wide.at[j], target.at[:, :, :, :, :, pl.ds(column * 1024, 1024)], local.at[j]
+
+    def event(j, number):
+        if not 0 <= j < 12:
+            return
+        if number == 0:
+            loads[j].wait()
+        chunks[j].step(number)
+        if number == 4:
+            if j < 8:
+                target = in_full if j < 3 else (out_full if j == 3 else up_full)
+                column = j if j < 3 else (0 if j == 3 else j - 4)
+                save(wide.at[j], target.at[:, :, :, :, :, pl.ds(column * 1024, 1024)])
+            else:
+                save(tall.at[j - 8], down_full.at[:, :, :, :, :, pl.ds(256 * (j - 8), 256)])
+
+    def weight(j, columns):
+        return wide[j, :, :, :, :, :, columns].reshape(width, columns.size)
+
+    images = Images(starts, p.seq, length)
+
+    def first_norm():
+        for y in range(2):
+            for x in range(2):
+                for k in range(2):
+                    value = pack[y, x, 2 * k : 2 * k + 2].astype(FULL)
+                    value = (value[0, 0] + value[0, 1]) + (value[1, 0] + value[1, 1])
+                    at = 128 * ((y * 2 + x) * 2 + k)
+                    gains[:, at : at + 128] = value
+        save(gains, gains_out)
+        loads[13].wait()
+
+        @pl.loop(0, length // 128)
+        def _(i):
+            rows = tile(i, 128)
+            value, _ = statistics(tokens[rows, :].astype(FULL))
+            normed[rows, :] = (value * gains[0:1, :] + gains[1:2, :]).astype(LOW)
+
+        mask[...] = same_mask(images, length, length, False)
+
+    def project(j):
+        @pl.loop(0, 2)
+        def _(i):
+            value = product(normed[...], weight(j, tile(i, 512)))
+            if j < 2:
+                value = jnp.where(value > 0, value + 1.0, jnp.exp(jnp.minimum(value, 0.0)))
+            heads[j, :, tile(i, 512)] = value.astype(LOW)
+
+    def update():
+        tail = images.tail.astype(LOW)
+
+        @pl.loop(0, 8)
+        def _(i):
+            lanes = tile(i, 128)
+            key = heads[1, :, lanes] * tail
+            square = down_rows(key, heads[2, :, lanes])
+            outgoing[i, 0:HEAD] = pack_pair(square).astype(LOW)
+            total = product(jnp.ones((16, length), LOW), key)
+            outgoing[i, HEAD : HEAD + 16] = total.astype(LOW)
+
+        save(heads, heads_out)
+        for copy in state:
+            copy.start()
+
+    state = [
+        remote(outgoing, incoming.at[d], state_send.at[d], state_recv.at[d], device)
+        for d, device in enumerate(p.following)
+    ]
+
+    def enter():
+        for copy in state:
+            copy.wait_recv()
+
+        @pl.loop(0, 8)
+        def _(i):
+            value = incoming[0, i].astype(FULL) + images.flag_before * incoming[1, i].astype(FULL)
+            memory[i] = value[0:HEAD].astype(LOW)
+            sums[i] = value[HEAD : HEAD + 8]
+
+        save(memory, memory_out)
+        save(sums, sums_out)
+
+    def attend(begin, end):
+        lanes_column = head_lanes(length)
+        blocks = own_block()
+        keep = images.keep.astype(LOW)
+        half = length // 2
+        identity = jnp.where(
+            lax.broadcasted_iota(jnp.int32, (128, 128), 0)
+            == lax.broadcasted_iota(jnp.int32, (128, 128), 1),
+            1.0,
+            0.0,
+        )
+        ones = jnp.ones((length, 128), LOW)
+
+        @pl.loop(begin, end)
+        def _(i):
+            lanes = tile(i, 128)
+            query, key, value = heads[0, :, lanes], heads[1, :, lanes], heads[2, :, lanes]
+            wider = jnp.concatenate([value, ones], axis=1)
+            parts = []
+            for h in range(2):
+                mine = lanes_column if h == 0 else ~lanes_column
+                own = jnp.where(mine, query, jnp.zeros_like(query))
+                upper = across(own[:half], key[:half]).astype(LOW) * mask[:half, :half]
+                lower = across(own[half:], key).astype(LOW) * mask[half:, :]
+                parts.append(
+                    jnp.concatenate([product(upper, wider[:half]), product(lower, wider)], axis=0)
+                )
+            diagonal = (identity * sums[i, 0:1]).astype(LOW)
+            right = jnp.concatenate(
+                [unpack_pair(memory[i]), product(diagonal, blocks).astype(LOW)], axis=1
             )
-        )
-    for j in range(4):
-        outs.append(
-            pltpu.make_async_copy(
-                tall.at[j], outputs[3].at[:, :, :, :, :, pl.ds(256 * j, 256)], local.at[8 + j]
+            carried = product(query * keep, right)
+            numerator = jnp.where(lanes_column, parts[0][:, :128], parts[1][:, :128])
+            denominator = jnp.where(lanes_column, parts[0][:, 128:], parts[1][:, 128:])
+            over = 1.0 / (denominator + carried[:, 128:])
+            value = (numerator + carried[:, :128]) * over
+            inverse[:, lanes] = over
+            mixed[:, lanes] = value
+            mixed_low[:, lanes] = value.astype(LOW)
+
+    def join():
+        save(mixed, mixed_out)
+        save(inverse, inverse_out)
+
+        @pl.loop(0, 2)
+        def _(i):
+            columns = tile(i, 512)
+            middle[:, columns] = tokens[:, columns].astype(FULL) + product(
+                mixed_low[...], weight(3, columns)
             )
-        )
+
+        save(middle, middle_out)
+
+    def second_norm():
+        @pl.loop(0, length // 128)
+        def _(i):
+            rows = tile(i, 128)
+            value, _ = statistics(middle[rows, :])
+            normed[rows, :] = (value * gains[2:3, :] + gains[3:4, :]).astype(LOW)
+
+    def raise_up(j):
+        @pl.loop(0, 4)
+        def _(i):
+            value = product(normed[...], weight(4 + j, tile(i, 256)))
+            columns = pl.ds(pl.multiple_of(j * 1024 + i * 256, 256), 256)
+            value, steep = gelu_both(value)
+            active[:, columns] = value.astype(LOW)
+            slope[:, columns] = steep.astype(LOW)
+
+        if j == 3:
+            save(slope, slope_out)
+
+    def down_gradient(begin, end):
+        if begin == 0:
+            loads[14].wait()
+
+        @pl.loop(begin, end)
+        def _(i):
+            value = down_rows(active[:, tile(i, 512)], cotangent[...]).astype(LOW)
+            y, x, z = i // 4, i // 2 % 2, i % 2 * 2
+            for j in range(4):
+                part = value[:, 256 * j : 256 * j + 256].reshape(2, 2, 128, 256)
+                grad_down[j, y, x, pl.ds(z, 2)] = part
+
+        if end == 8:
+            save(grad_down, grad_down_out)
+
+    def lower(j):
+        columns = slice(256 * j, 256 * j + 256)
+
+        @pl.loop(0, 2)
+        def _(i):
+            rows = tile(i, 256)
+            value = product(active[rows, :], tall[j].reshape(4 * width, 256))
+            result[rows, columns] = (middle[rows, columns] + value).astype(LOW)
+
+        save(result.at[:, pl.ds(256 * j, 256)], result_out.at[:, pl.ds(256 * j, 256)])
+
+    work = {
+        5: [functools.partial(project, 0)],
+        6: [functools.partial(project, 1)],
+        7: [functools.partial(project, 2), update],
+        8: [enter, functools.partial(attend, 0, 2), functools.partial(attend, 2, 4)],
+        9: [
+            functools.partial(attend, 4, 6),
+            functools.partial(attend, 6, 8),
+            join,
+        ],
+        10: [second_norm, functools.partial(raise_up, 0), functools.partial(raise_up, 1)],
+        11: [functools.partial(raise_up, 2)],
+        12: [
+            functools.partial(raise_up, 3),
+            functools.partial(down_gradient, 0, 4),
+            functools.partial(down_gradient, 4, 8),
+        ],
+        13: [functools.partial(lower, 0)],
+        14: [functools.partial(lower, 1)],
+        15: [functools.partial(lower, 2)],
+    }
     for tick in range(12 + 4):
-        for number in range(5):
-            j = tick - number
-            if 0 <= j < 12:
-                chunks[j].step(number)
-                if number == 4:
-                    outs[j].start()
-        if tick < 5:
-            small.step(tick)
-    outputs[4][...] = pack[...]
+        todo = work.get(tick, []) + [lambda: None] * 3
+        if tick == 0:
+            event(0, 0)
+            loads[12].wait()
+            small.step(0)
+            event(1, 0)
+            for number in range(1, 5):
+                small.step(number)
+            first_norm()
+            continue
+        if tick > 1:
+            event(tick, 0)
+        event(tick - 1, 1)
+        todo[0]()
+        event(tick - 2, 2)
+        todo[1]()
+        event(tick - 3, 3)
+        event(tick - 4, 4)
+        todo[2]()
+    lower(3)
     small.finish()
+    for copy in state:
+        copy.wait_send()
     for chunk in chunks:
         chunk.finish()
-    for copy in outs:
+    for copy in stores:
         copy.wait()
 
 
-def gather_all(in_weight, out_weight, up_weight, down_weight, pack):
+def forward_pass(tokens, cotangent, starts, in_weight, out_weight, up_weight, down_weight, pack):
+    length, width = tokens.shape
     block = lambda rows, columns: jax.ShapeDtypeStruct((2, 2, 4, 2, rows, columns), LOW)
+    shape = jax.ShapeDtypeStruct
 
     def body(*refs):
-        gather_kernel(refs[:5], refs[5:10], *refs[10:])
+        forward_kernel(refs[:8], refs[8:22], refs[22:])
 
     return pl.pallas_call(
         body,
-        out_shape=[block(32, 3072), block(32, 1024), block(32, 4096), block(128, 1024), block(16, 128)],
-        in_specs=[pl.BlockSpec(memory_space=pltpu.VMEM)] * 5,
-        out_specs=[pl.BlockSpec(memory_space=pl.ANY)] * 4 + [pl.BlockSpec(memory_space=pltpu.VMEM)],
+        out_shape=[
+            block(32, 3072),
+            block(32, 1024),
+            block(32, 4096),
+            block(128, 1024),
+            shape((4, 2, 2, 4, 2, 128, 256), LOW),
+            shape((length, width), LOW),
+            shape((3, length, width), LOW),
+            shape((length, width), FULL),
+            shape((length, width), FULL),
+            shape((length, width), FULL),
+            shape((length, 4 * width), LOW),
+            shape((8, HEAD, 128), LOW),
+            shape((8, 8, 128), FULL),
+            shape((16, width), FULL),
+        ],
+        in_specs=[
+            pl.BlockSpec(memory_space=pltpu.SMEM if i == 2 else pl.ANY) for i in range(8)
+        ],
+        out_specs=[pl.BlockSpec(memory_space=pl.ANY)] * 14,
         scratch_shapes=[
             pltpu.VMEM((8, 2, 2, 4, 2, 32, 1024), LOW),
             pltpu.VMEM((4, 2, 2, 4, 2, 128, 256), LOW),
             pltpu.VMEM((2, 2, 4, 2, 16, 128), LOW),
+            pltpu.VMEM((length, width), LOW),
+            pltpu.VMEM((length, width), LOW),
+            pltpu.VMEM((16, width), FULL),
+            pltpu.VMEM((length, width), LOW),
+            pltpu.VMEM((3, length, width), LOW),
+            pltpu.VMEM((length, length), LOW),
+            pltpu.VMEM((length, width), FULL),
+            pltpu.VMEM((length, width), LOW),
+            pltpu.VMEM((length, width), FULL),
+            pltpu.VMEM((length, width), FULL),
+            pltpu.VMEM((length, 4 * width), LOW),
+            pltpu.VMEM((length, 4 * width), LOW),
+            pltpu.VMEM((4, 2, 2, 4, 2, 128, 256), LOW),
+            pltpu.VMEM((length, width), LOW),
+            pltpu.VMEM((8, HEAD + 16, 128), LOW),
+            pltpu.VMEM((2, 8, HEAD + 16, 128), LOW),
+            pltpu.VMEM((8, HEAD, 128), LOW),
+            pltpu.VMEM((8, 8, 128), FULL),
             pltpu.SemaphoreType.DMA((12, 11)),
             pltpu.SemaphoreType.DMA((12, 11)),
             pltpu.SemaphoreType.DMA((9,)),
             pltpu.SemaphoreType.DMA((9,)),
-            pltpu.SemaphoreType.DMA((12,)),
+            pltpu.SemaphoreType.DMA((2,)),
+            pltpu.SemaphoreType.DMA((2,)),
+            pltpu.SemaphoreType.DMA((15,)),
+            pltpu.SemaphoreType.DMA((26,)),
         ],
         compiler_params=pltpu.CompilerParams(
-            collective_id=0, has_side_effects=True, vmem_limit_bytes=60 << 20
+            collective_id=0, has_side_effects=True, vmem_limit_bytes=62 << 20
         ),
-        name="gather_weights",
-    )(in_weight, out_weight, up_weight, down_weight, pack)
+        name="forward_pass",
+    )(tokens, cotangent, starts, in_weight, out_weight, up_weight, down_weight, pack)
 
 
 def scatter_kernel(inputs, outputs, wide, tall, send, recv):
@@ -615,37 +1039,6 @@
         ),
         name="scatter_gradients",
     )(*[grad.reshape(2, 2, 4, 2, grad.shape[0] // 32, grad.shape[1]) for grad in grads])
-
-
-class SmallGather(Gather):
-    def __init__(self, place, full, send, recv):
-        p = place
-        own = full.at[p.y, p.x, p.z, p.c]
-        parts = [(own, device) for device in p.along_z]
-        parts.append((full.at[p.y, p.x, :, p.c], p.over_x))
-        parts.append((full.at[p.y, :, :, p.c], p.over_y))
-        for y in range(2):
-            for x in range(2):
-                parts.append((full.at[y, x, :, p.c], p.sibling))
-        self.copies = [
-            remote(ref, ref, send.at[i], recv.at[i], device)
-            for i, (ref, device) in enumerate(parts)
-        ]
-
-    def step(self, number):
-        if number == 0:
-            self.start(0, 1, 2)
-        elif number == 1:
-            self.arrive(0, 1, 2)
-            self.start(3)
-        elif number == 2:
-            self.arrive(3)
-            self.start(4)
-        elif number == 3:
-            self.arrive(4)
-            self.start(5, 6, 7, 8)
-        else:
-            self.arrive(5, 6, 7, 8)
 
 
 def on_device(
@@ -677,94 +1070,62 @@
     mine = lax.axis_index("dp") * 8 + lax.axis_index("seq")
     pack = jnp.stack([first_gain, first_shift, second_gain, second_shift]).astype(FULL)
     pack = jnp.roll(jnp.pad(pack, ((0, 12), (0, 96))), 32 * (mine % 4), axis=1).astype(LOW)
-    in_full, out_full, up_full, down_full, packs = gather_all(
+    (
+        in_full,
+        out_full,
+        up_full,
+        down_full,
+        grad_down,
+        result,
+        heads,
+        mixed,
+        inverse,
+        middle_tokens,
+        slope,
+        memory,
+        sums,
+        gains,
+    ) = forward_pass(
+        tokens[0],
+        cotangent[0],
+        starts,
         query_key_value_weight,
         attention_output_weight,
         up_projection_weight,
         down_projection_weight,
         pack,
     )
+    result_tokens = result.reshape(1, local_len, model_width)
     in_full, out_full = in_full.reshape(1024, 3072), out_full.reshape(1024, 1024)
     up_full, down_full = up_full.reshape(1024, 4096), down_full.reshape(4096, 1024)
-    packs = jnp.sum(packs.reshape(8, 4, 16, 128).astype(FULL), axis=1)
-    packs = jnp.transpose(packs[:, :4], (1, 0, 2)).reshape(4, 1024)
-    gain_one, shift_one, gain_two, shift_two = packs[0], packs[1], packs[2], packs[3]
-    first_normed_tokens = layer_norm(input_tokens, gain_one, shift_one)
-    normed_low = first_normed_tokens.astype(jnp.bfloat16)
+    gain_one, shift_one, gain_two, shift_two = gains[0], gains[1], gains[2], gains[3]
+    normed_low = layer_norm(input_tokens, gain_one, shift_one).astype(LOW)
     projected_tokens = jnp.dot(normed_low, in_full, preferred_element_type=jnp.float32)
     queries = projected_tokens[:, :model_width]
     keys_raw = projected_tokens[:, model_width : 2 * model_width]
-    values_raw = projected_tokens[:, 2 * model_width :]
-    feat_query = feature(queries).astype(jnp.bfloat16).reshape(block_shape)
-    feat_key = feature(keys_raw).astype(jnp.bfloat16).reshape(block_shape)
-    value_low = values_raw.astype(jnp.bfloat16).reshape(block_shape)
-    block_number = 0
+    feat_query, feat_key, value_low = heads[0].reshape(block_shape), heads[1].reshape(block_shape), heads[2].reshape(block_shape)
     last_id = image_ids[-1]
     tail_mask = image_ids == last_id
-    tail_key = jnp.where(tail_mask[:, None, None], feat_key[block_number], zero_low)
     keep_list = [image_ids == before_id]
     tail_list = [tail_mask]
     flag_list = [(last_id == before_id).astype(jnp.float32)]
     same_list = [causal & (image_ids[:, None] == image_ids[None, :])]
-    update_list = [
-        jnp.einsum(
-            "jhe,jhf->hef", tail_key, value_low[block_number], preferred_element_type=jnp.float32
-        )
-    ]
-    total_list = [jnp.sum(tail_key.astype(jnp.float32), axis=0)]
     identity = (
         jnp.ones((), jnp.float32),
         jnp.zeros((head_count, HEAD, HEAD), jnp.float32),
         jnp.zeros((head_count, HEAD), jnp.float32),
     )
-    combined = identity
-    block_number = 0
-    combined = combine(
-        combined, (flag_list[block_number], update_list[block_number], total_list[block_number])
-    )
-    entering = prefix(combined, "seq", combine, identity, False)
-    memory = entering[1]
-    key_sum = entering[2]
-    block_number = 0
-    query_block = feat_query[block_number]
-    keep_float = keep_list[block_number].astype(jnp.float32)
-    memory_low = memory.astype(jnp.bfloat16)
-    raw_scores = jnp.einsum(
-        "the,jhe->htj", query_block, feat_key[block_number], preferred_element_type=jnp.float32
-    )
-    masked = jnp.where(same_list[block_number][None], raw_scores, 0.0)
-    scores_low = masked.astype(jnp.bfloat16)
-    carried = (
-        jnp.einsum("the,hef->thf", query_block, memory_low, preferred_element_type=jnp.float32)
-        * keep_float[:, None, None]
-    )
-    numerator = (
-        jnp.einsum(
-            "htj,jhf->thf", scores_low, value_low[block_number], preferred_element_type=jnp.float32
-        )
-        + carried
-    )
-    denominator = jnp.transpose(jnp.sum(masked, axis=2)) + keep_float[:, None] * jnp.sum(
-        query_block.astype(jnp.float32) * key_sum[None], axis=2
-    )
-    memory_list = [memory_low]
-    keysum_list = [key_sum]
-    numer_list = [numerator]
-    denom_list = [denominator]
-    ratio_list = numerator / denominator[:, :, None]
-    mixed_low = ratio_list.reshape(local_len, model_width).astype(jnp.bfloat16)
-    middle_tokens = input_tokens + jnp.dot(mixed_low, out_full, preferred_element_type=jnp.float32)
+    memory_list = [jnp.transpose(memory.reshape(8, HEAD, 2, HEAD), (0, 2, 1, 3)).reshape(16, HEAD, HEAD)]
+    keysum_list = [sums[:, 0].reshape(16, HEAD)]
+    denominator = 1.0 / inverse.reshape(512, 16, 64)
+    numer_list = [mixed.reshape(512, 16, 64) * denominator]
+    denom_list = [denominator[:, :, 0]]
+    mixed_low = mixed.astype(LOW)
     normed_two_low = layer_norm(middle_tokens, gain_two, shift_two).astype(jnp.bfloat16)
-    upper_hidden = jnp.dot(normed_two_low, up_full, preferred_element_type=jnp.float32)
-    active_low = jax.nn.gelu(upper_hidden).astype(jnp.bfloat16)
-    result = middle_tokens + jnp.dot(active_low, down_full, preferred_element_type=jnp.float32)
-    result_tokens = result.astype(jnp.bfloat16).reshape(1, local_len, model_width)
     grad_out = cotangent[0].astype(jnp.float32)
     grad_out_low = cotangent[0]
-    grad_down = rows_product(active_low, grad_out_low)
     d_active = cols_product(grad_out_low, down_full)
-    gelu_value, gelu_back = jax.vjp(jax.nn.gelu, upper_hidden)
-    g_upper = gelu_back(d_active)[0].astype(jnp.bfloat16)
+    g_upper = (slope.astype(FULL) * d_active).astype(jnp.bfloat16)
     grad_up = rows_product(normed_two_low, g_upper)
     d_normed_two = cols_product(g_upper, up_full)
     norm_value, norm_back = jax.vjp(layer_norm, middle_tokens, gain_two, shift_two)
@@ -867,7 +1228,7 @@
         grad_in_weight.astype(LOW),
         grad_out_weight.astype(LOW),
         grad_up.astype(LOW),
-        grad_down.astype(LOW),
+        jnp.moveaxis(grad_down, 0, 5).reshape(4096, 1024),
     )
     summed = (
         *weights,

time: 584 us -> 528 us (0.904)
  matrix products: 127 us -> 84.2 us
  blocking collectives: 88.3 us -> 69.7 us
  Pallas kernels: 243 us -> 256 us
  other arithmetic: 45.7 us -> 33.1 us
  local copies, waits for them, and re-layouts: 45.1 us -> 53.2 us
    dot_general x7 -> x0, matrix products: 34.4 us -> none  [the longest x1 12 us: on_device(): jnp.dot(active_low, down_full, preferred_element_type=jnp.float32)]
    all_gather x2 -> x1, blocking collectives: 28.3 us -> 14.2 us  [prefix(): lax.all_gather(part.astype(kind), axis)]
    pallas_call x1, Pallas kernels: 124 us -> 135 us  [forward_pass(): pl.pallas_call(body, out_shape=[block(32, 3072), block(32, 1024), block(3...]
    select_n x32 -> x16, other arithmetic: 20.7 us -> 10.3 us  [lap(): return jax.tree.map(lambda a, b: jnp.where(reached, a, b), new, before)]
    another operation x0 -> x1, local copies, waits for them, and re-layouts: none -> 7.81 us  [scatter_all(): grad.reshape(2, 2, 4, 2, grad.shape[0] // 32, grad.shape[1])]
    dot_general x4 -> x3, matrix products: 29.4 us -> 21.7 us  [rows_product(): lax.dot_general(factor_one, factor_two, (((0,), (0,)), ((), ())), preferr...]
    slice x2 -> x7, local copies, waits for them, and re-layouts: 1.89 us -> 8.42 us  [the longest x2 3.19 us: on_device(): heads[2].reshape(block_shape)]
    unnamed x53 -> x102, local copies, waits for them, and re-layouts: 17.3 us -> 12.8 us
  transfers between devices with their start and end apart: 2 -> 1, of which waited for: 0 -> 0; matrix products, arithmetic and copies ran while one was open for 9% -> 14% of each run, Pallas kernels for 0% -> 0%
where the time goes in v2:
time: 528 us; the launch traced here: 518 us
  Pallas kernels  256 us (48%)
  matrix products  84.2 us (16%)
  blocking collectives  69.7 us (13%)
  local copies, waits for them, and re-layouts  53.2 us (10%)
  other arithmetic  33.1 us (6%)
  between operations  16.3 us (3%)
  loops' own time  5.8 us (1%)
    pallas_call x1, Pallas kernels, forward_pass(): pl.pallas_call(body, out_shape=[block(32, 3072), block(32, 1024), block(3...  135 us
    pallas_call x1, Pallas kernels, scatter_all(): pl.pallas_call(body, out_shape=[jax.ShapeDtypeStruct(shape, FULL) for sha...  121 us
    unnamed x2, blocking collectives  55.5 us
    dot_general x4, matrix products, cols_product(): lax.dot_general(factor_one, factor_two, (((1,), (1,)), ((), ())), preferr...  23.5 us
    dot_general x3, matrix products, rows_product(): lax.dot_general(factor_one, factor_two, (((0,), (0,)), ((), ())), preferr...  21.7 us
    all_gather x1, blocking collectives, prefix(): lax.all_gather(part.astype(kind), axis)  14.2 us
    unnamed x102, local copies, waits for them, and re-layouts  12.8 us
  transfers between devices with their start and end apart: 1, of which 0 were waited for; matrix products, arithmetic and copies ran while one was open for 14% of the time, Pallas kernels for 0%

profile of v2, /device:TPU:0, one launch (start us, length us, event | category | flops | bytes accessed | tf_op | source)
XLA Modules:
  0.0 518.2 jit_solution(449299095120090113)
XLA Ops:
  8.7 134.8 %forward_pass.1 = (bf16[2,2,4,2,32,3072]{5,4,3,2,1,0:T(8,128)(2,1)}, bf16[2,2,4,2,32,1024]{5,4,3,2,1,0:T(8,128)(2,1)}, bf16[2,2,4,2,32,4096]{5,4,3,2,1,0:T(8,128...) custom-call(bf16[512,1024]{1,0:T(8,128)(2,1)} %bitcast.128, ...), custom_call_target="tpu_custom_call" | custom-call | tf_op jit(solution)/shard_map/forward_pass/pallas_call | solution.py:918
  143.5 1.9 reduce_sum.140
  145.7 3.7 multiply_reduce_fusion.4
  149.4 1.5 fusion.83
  150.9 8.9 %fusion.2 = bf16[512,4096]{1,0:T(8,128)(2,1)S(1)} fusion(bf16[512,4096]{1,0:T(8,128)(2,1)} %get-tuple-element.206, bf16[4096,1024]{1,0:T(8,128)(2,1)} %bitcast.173, bf16[1,512,1024]{2,1,0:T(8,128)(2,1)S(1)} %copy-done.6), kind=kOutput, calls=%fused_computation.7 | convolution fusion | flops 4301258752 | bytes 17825792 | tf_op jit(solution)/shard_map/dot_general | solution.py:64
  159.9 6.8 %multiply_reduce_fusion = (f32[1024]{0:T(1024)}, f32[512]{0:T(512)S(1)}, f32[1024]{0:T(1024)}, f32[512,1024]{1,0:T(8,128)}) fusion(f32[512,1024]{1,0:T(8,128)S(1)} %copy-done.3, f32[512]{0:T(512)S(1)} %fusion.64, f32[512]{0:T(512)S(1)} %broadcast_multiply_fusion.1, f32[1024]{0:T(1024)S(1)} %bitcast.159, bf16[512,4096]{1,0:T(8,128)(2,1)S(1)} %fusion.2, ...), kind=kOutput, calls=%fused_computation.35 | convolution fusion | flops 4299159040 | bytes 16795648 | tf_op jit(solution)/shard_map/dot_general | solution.py:64
  166.7 2.9 copy.73
  169.6 2.9 copy.71
  172.5 2.4 fusion.80
  178.3 1.4 multiply_reduce_fusion.2
  180.2 1.7 fusion.81
  181.9 1.5 copy.77
  185.7 1.3 fusion.78
  189.9 4.6 convolution_convert_fusion.2
  194.5 1.3 copy.70
  195.8 1.6 mul.272
  197.4 3.0 copy.78
  200.5 1.7 fusion.84
  202.2 1.5 copy.72
  205.6 2.7 add_convert_fusion
  208.4 3.5 fusion.3
  213.1 8.3 %fusion.20 = f32[512,16,64]{0,2,1:T(8,128)} fusion(f32[16,64,512]{2,1,0:T(8,128)} %fusion.84, bf16[512,16,64]{0,2,1:T(8,128)(2,1)} %bitcast.138, bf16[16,512,512]{2,1,0:T(8,128)(2,1)} %copy-done.10, pred[512,512]{1,0:T(8,128)(4,1)S(1)} %fusion.44, f32[16,64]{1,0:T(8,128)S(1)} %mul.273, f32[512,16]{0,1:T(8,128)S(1)} %bitcast.152, f32[512]{0:T(512)S(1)} %copy-done.39), kind=kOutput, calls=%fused_computation.34 | convolution fusion | flops 543162368 | bytes 13932544 | tf_op jit(solution)/shard_map/htj,jhe->the/dot_general | solution.py:1183
  221.4 8.4 %fusion.24 = f32[512,3072]{1,0:T(8,128)} fusion(bf16[1024,3072]{1,0:T(8,128)(2,1)} %bitcast.174, bf16[1,512,1024]{2,1,0:T(8,128)(2,1)S(1)} %copy-done, f32[1024]{0:T(1024)S(1)} %bitcast.162, f32[1024]{0:T(1024)S(1)} %bitcast.154, f32[512]{0:T(512)S(1)} %fusion.65, f32[512]{0:T(512)S(1)} %broadcast_multiply_fusion), kind=kOutput, calls=%fused_computation.56 | convolution fusion | flops 3224371200 | bytes 13643776 | tf_op jit(solution)/shard_map/dot_general | solution.py:1103
  229.8 1.6 multiply_reduce_fusion.1
  231.4 16.3 %all-reduce.1 = bf16[8]{0:T(256)(128)(2,1)S(1)} all-reduce(bf16[8]{0:T(256)(128)(2,1)S(1)} %dynamic-update-slice), channel_id=1, replica_groups=mesh['dp'=4,'seq'=8] {'seq'}, use_global_device_ids=true, to_apply=%add.1 | all-reduce | flops 8 | bytes 32
  247.8 3.0 copy.75
  250.8 7.8 %copy.88 = bf16[4,2,2,4,2,16,8,256]{7,6,0,5,4,3,2,1:T(8,128)(2,1)} copy(bf16[4,2,2,4,2,16,8,256]{7,6,5,4,3,2,1,0:T(8,128)(2,1)} %bitcast.134) | data formatting | bytes 16777216 | tf_op jit(solution)/shard_map/reshape;reshape | solution.py:1041
  258.6 14.2 %all_gather.20 = bf16[8,16,64]{2,1,0:T(8,128)(2,1)S(1)} all-gather(bf16[1,16,64]{2,1,0:T(8,128)(2,1)S(1)} %convert_element_type.165), channel_id=1, replica_groups=mesh['dp'=4,'seq'=8] {'seq'}, dimensions={0}, use_global_device_ids=true | all-gather | bytes 18432 | tf_op jit(solution)/shard_map/all_gather | solution.py:17
  272.8 6.8 %fusion.7 = f32[16,64,512]{2,1,0:T(8,128)} fusion(bf16[512,16,64]{0,2,1:T(8,128)(2,1)S(1)} %divide_convert_fusion, bf16[512,16,64]{0,2,1:T(8,128)(2,1)} %bitcast.146, bf16[512,16,64]{0,2,1:T(8,128)(2,1)} %bitcast.139, pred[512,512]{1,0:T(8,128)(4,1)S(1)} %fusion.44), kind=kOutput, calls=%fused_computation.18 | convolution fusion | flops 1082130432 | bytes 5505024 | tf_op jit(solution)/shard_map/htj,thf->jhf/dot_general | solution.py:1203
  279.6 10.8 %convolution_convert_fusion = bf16[1024,4096]{1,0:T(8,128)(2,1)} fusion(bf16[512,4096]{1,0:T(8,128)(2,1)} %copy-done.41, f32[512,1024]{1,0:T(8,128)} %get-tuple-element.210, f32[1024]{0:T(1024)S(1)} %bitcast.164, f32[512]{0:T(512)S(1)} %copy-done.28, f32[512]{0:T(512)S(1)} %broadcast_multiply_fusion.1, f32[1024]{0:T(1024)S(1)} %bitcast.161), kind=kOutput, calls=%fused_computation.9 | convolution fusion | flops 4301783040 | bytes 14692352 | tf_op jit(solution)/shard_map/dot_general | solution.py:58
  290.4 20.8 %while.18 = (s32[]{:T(128)}, f32[16,64,64]{2,1,0:T(8,128)S(1)}, f32[16,64]{1,0:T(8,128)S(1)}, s32[]{:T(128)}, bf16[8]{0:T(256)(128)(2,1)S(1)}, /*index=5*/bf16[8...) while((s32[]{:T(128)}, f32[16,64,64]{2,1,0:T(8,128)S(1)}, ...), condition=%wide.region_11.12_spmd.clone, body=%wide.region_10.11_spmd.clone.sunk | while | flops 332809 | bytes 665815 | solution.py:35
  291.9 1.3 fusion.106
  294.5 1.3 fusion.106
  297.1 1.3 fusion.106
  299.6 1.3 fusion.106
  302.2 1.3 fusion.106
  304.8 1.3 fusion.106
  307.4 1.3 fusion.106
  311.3 3.0 add_convert_fusion.2
  314.3 2.4 copy.82
  316.7 3.4 multiply_add_fusion
  320.1 3.1 copy.79
  323.2 4.2 add_convert_fusion.4
  327.4 6.4 %fusion.77 = (f32[1024]{0:T(1024)S(1)}, f32[512]{0:T(512)S(1)}, f32[512,1024]{1,0:T(8,128)S(1)}) fusion(f32[1024]{0:T(1024)S(1)} %bitcast.155, f32[512]{0:T(512)S(1)} %broadcast_multiply_fusion, bf16[1,512,1024]{2,1,0:T(8,128)(2,1)S(1)} %copy-done, bf16[1024,3072]{1,0:T(8,128)(2,1)} %bitcast.175, bf16[512,1024]{1,0:T(8,128)(2,1)S(1)} %copy-done.21, ...), kind=kOutput, calls=%fused_computation.135 | convolution fusion | flops 3233806848 | bytes 12595200 | tf_op jit(solution)/shard_map/dot_general | solution.py:64
  333.9 6.3 %convolution_convert_fusion.1 = bf16[1024,3072]{1,0:T(8,128)(2,1)} fusion(bf16[512,1024]{1,0:T(8,128)(2,1)S(1)} %copy-done.21, bf16[512,1024]{1,0:T(8,128)(2,1)S(1)} %get-tuple-element.281, bf16[512,1024]{1,0:T(8,128)(2,1)S(1)} %get-tuple-element.280, f32[1024]{0:T(1024)S(1)} %bitcast.163, f32[512]{0:T(512)S(1)} %fusion.65, f32[1024]{0:T(1024)S(1)} %bitcast.156, ...), kind=kOutput, calls=%fused_computation.12 | convolution fusion | flops 3236954112 | bytes 10498048 | tf_op jit(solution)/shard_map/dot_general | solution.py:58
  342.0 2.2 add_bitcast_fusion
  344.3 120.9 %scatter_gradients.1 = (f32[32,3072]{1,0:T(8,128)}, f32[32,1024]{1,0:T(8,128)}, f32[32,4096]{1,0:T(8,128)}, f32[128,1024]{1,0:T(8,128)}) custom-call(bf16[2,2,4,2,32,3072]{5,4,3,2,1,0:T(8,128)(2,1)} %bitcast.137, bf16[2,2,4,2,32,1024]{5,4,3,2,1,0:T(8,128)(2,1)} %bitcast.143, bf16[2,2,4,2,32,4096]{5,4,3,2,1,0:T(8,128)(2,1)} %bitcast.133, ...), custom_call_target="tpu_custom_call" | custom-call | tf_op jit(solution)/shard_map/scatter_gradients/pallas_call | solution.py:1026
  465.3 39.2 %all-reduce.6 = (f32[1024]{0:T(1024)S(1)}, f32[1024]{0:T(1024)S(1)}, f32[1024]{0:T(1024)S(1)}, f32[1024]{0:T(1024)S(1)}) all-reduce(f32[1024]{0:T(1024)S(1)} %get-tuple-element.251, f32[1024]{0:T(1024)S(1)} %get-tuple-element.254, f32[1024]{0:T(1024)S(1)} %copy-done.31, ...), channel_id=3, replica_groups=mesh['dp'=4,'seq'=8] {'dp','seq'}, use_global_device_ids=true, to_apply=%region_15.16.clone | all-reduce | flops 4096 | bytes 32768
  (155 shorter events, 27.1 us)
Async XLA Ops:
  7.2 283.2 %all-gather.3.cloned.1.call-start = ((), (), s32[]{:S(2)}) async-start(), calls=%async_computation | async-start | bytes 2359296 | tf_op jit(solution)/shard_map/all_gather | solution.py:17
  143.5 2.2 copy-start.3
  145.7 5.2 %copy-start.6 = (bf16[1,512,1024]{2,1,0:T(8,128)(2,1)S(1)}, bf16[1,512,1024]{2,1,0:T(8,128)(2,1)}, u32[]{:S(2)}) copy-start(bf16[1,512,1024]{2,1,0:T(8,128)(2,1)} %param.23) | copy-start | bytes 3145732
  145.7 14.2 %slice-start = ((s8[8388608]{0:T(1024)(128)(4,1)}), s8[4194304]{0:T(1024)(128)(4,1)S(1)}, s32[]{:S(2)}) async-start(s8[8388608]{0:T(1024)(128)(4,1)} %bitcast.170), calls=%async_computation.1 | async-start | bytes 8388608
  149.4 23.1 %copy-start.27 = (f32[512]{0:T(512)}, f32[512]{0:T(512)S(1)}, u32[]{:S(2)}) copy-start(f32[512]{0:T(512)S(1)} %fusion.64) | copy-start | bytes 6148
  150.9 9.0 %slice-start.1 = ((s8[8388608]{0:T(1024)(128)(4,1)}), s8[4194304]{0:T(1024)(128)(4,1)S(1)}, s32[]{:S(2)}) async-start(s8[8388608]{0:T(1024)(128)(4,1)} %bitcast.170), calls=%async_computation.2 | async-start | bytes 8388608
  159.9 6.8 %copy-start.41 = (bf16[512,4096]{1,0:T(8,128)(2,1)}, bf16[512,4096]{1,0:T(8,128)(2,1)S(1)}, u32[]{:S(2)}) copy-start(bf16[512,4096]{1,0:T(8,128)(2,1)S(1)} %fusion.2) | copy-start | bytes 12582916
  172.5 3.7 copy-start.17
  174.9 1.3 copy-start.1
  174.9 2.5 copy-start.4
  174.9 3.3 copy-start.5
  176.2 3.4 copy-start.16
  178.3 1.9 copy-start.13
  181.9 1.5 copy-start.35
  184.8 2.2 copy-start.19
  185.7 2.5 copy-start
  187.0 2.0 copy-start.37
  189.9 4.6 copy-start.29
  189.9 4.6 copy-start.15
  197.4 3.0 copy-start.24
  202.2 2.8 copy-start.40
  203.7 4.6 copy-start.8
  205.6 2.7 copy-start.20
  208.3 4.0 copy-start.10
  208.3 4.7 copy-start.39
  213.1 8.3 %copy-start.33 = (f32[1,1024]{1,0:T(1,128)S(1)}, f32[1,1024]{1,0:T(1,128)}, u32[]{:S(2)}) copy-start(f32[1,1024]{1,0:T(1,128)} %get-tuple-element.290) | copy-start | bytes 12292
  221.4 8.5 %copy-start.12 = (f32[1,512,1024]{2,1,0:T(8,128)S(1)}, f32[1,512,1024]{2,1,0:T(8,128)}, u32[]{:S(2)}) copy-start(f32[1,512,1024]{2,1,0:T(8,128)} %copy.78) | copy-start | bytes 6291460
  221.4 8.5 %copy-start.38 = (pred[512]{0:T(512)(128)(4,1)S(1)}, pred[512]{0:T(512)(128)(4,1)}, u32[]{:S(2)}) copy-start(pred[512]{0:T(512)(128)(4,1)} %copy-done.37) | copy-start | bytes 1540
  272.8 6.8 %copy-start.28 = (f32[512]{0:T(512)S(1)}, f32[512]{0:T(512)}, u32[]{:S(2)}) copy-start(f32[512]{0:T(512)} %copy-done.27) | copy-start | bytes 6148
  272.8 6.8 %copy-start.34 = (f32[1,1024]{1,0:T(1,128)S(1)}, f32[1,1024]{1,0:T(1,128)}, u32[]{:S(2)}) copy-start(f32[1,1024]{1,0:T(1,128)} %get-tuple-element.289) | copy-start | bytes 12292
  290.4 20.9 %copy-start.14 = (bf16[1,512,1024]{1,2,0:T(8,128)(2,1)S(1)}, bf16[1,512,1024]{1,2,0:T(8,128)(2,1)}, u32[]{:S(2)}) copy-start(bf16[1,512,1024]{1,2,0:T(8,128)(2,1)} %copy.70) | copy-start | bytes 3145732
  290.4 20.9 %copy-start.36 = (pred[512]{0:T(512)(128)(4,1)S(1)}, pred[512]{0:T(512)(128)(4,1)}, u32[]{:S(2)}) copy-start(pred[512]{0:T(512)(128)(4,1)} %get-tuple-element.294) | copy-start | bytes 1540
  314.3 2.4 copy-start.9
  314.3 2.4 copy-start.30
  320.1 3.1 copy-start.11
  323.2 4.2 copy-start.21
  340.2 1.6 copy-start.2
  340.2 1.9 copy-start.7
  344.3 121.0 %copy-start.31 = (f32[1024]{0:T(1024)S(1)}, f32[1024]{0:T(1024)}, u32[]{:S(2)}) copy-start(f32[1024]{0:T(1024)} %get-tuple-element.249) | copy-start | bytes 12292
  344.3 121.0 %copy-start.32 = (f32[1024]{0:T(1024)S(1)}, f32[1024]{0:T(1024)}, u32[]{:S(2)}) copy-start(f32[1024]{0:T(1024)} %get-tuple-element.253) | copy-start | bytes 12292
  344.3 162.6 %copy-start.18 = (bf16[512,1024]{1,0:T(8,128)(2,1)S(1)}, bf16[512,1024]{1,0:T(8,128)(2,1)}, u32[]{:S(2)}) copy-start(bf16[512,1024]{1,0:T(8,128)(2,1)} %get-tuple-element.205) | copy-start | bytes 3145732
  465.2 42.6 %copy-start.25 = (f32[32,3072]{1,0:T(8,128)S(1)}, f32[32,3072]{1,0:T(8,128)}, u32[]{:S(2)}) copy-start(f32[32,3072]{1,0:T(8,128)} %get-tuple-element.389) | copy-start | bytes 1179652
  465.2 43.3 %copy-start.26 = (f32[32,1024]{1,0:T(8,128)S(1)}, f32[32,1024]{1,0:T(8,128)}, u32[]{:S(2)}) copy-start(f32[32,1024]{1,0:T(8,128)} %get-tuple-element.390) | copy-start | bytes 393220
  465.2 44.0 %copy-start.23 = (f32[32,4096]{1,0:T(8,128)S(1)}, f32[32,4096]{1,0:T(8,128)}, u32[]{:S(2)}) copy-start(f32[32,4096]{1,0:T(8,128)} %get-tuple-element.391) | copy-start | bytes 1572868
  506.8 3.2 copy-start.22
Sparse Core Ops, SparseCore 0:
  188.3 28.5 all-gather.2

commit v3 on v2

--- a/solution.py
+++ b/solution.py
@@ -411,8 +411,9 @@
 
 
 class Scatter:
-    def __init__(self, place, own, total, pair, first_a, first_b, second_a, second_b, last, send, recv):
+    def __init__(self, place, own, total, pair, first_a, first_b, second_a, second_b, last, send, recv, outside):
         p = place
+        self.outside, self.released = outside, False
         half = own.shape[4] // 2
         self.place, self.half = p, half
         self.own, self.total, self.pair = own, total, pair
@@ -427,7 +428,8 @@
             (total.at[p.y, 1 - p.x, :, low], second_a, p.over_x),
             (total.at[1 - p.y, p.x, :, high], second_b, p.over_y),
         ]
-        self.keep = pltpu.make_async_copy(own.at[:, :, :, p.c], total, send.at[8])
+        if outside:
+            self.keep = pltpu.make_async_copy(own.at[:, :, :, p.c], total, send.at[8])
         for d in (1, 2, 3):
             parts.append((total.at[p.y, p.x, (p.z + d) % 4], last.at[d - 1], p.along_z[d - 1]))
         self.copies = [
@@ -441,15 +443,18 @@
         total = self.total
         if number == 0:
             self.copies[0].start()
-            self.keep.start()
+            if self.outside:
+                self.keep.start()
         elif number == 1:
-            self.keep.wait()
+            if self.outside:
+                self.keep.wait()
             self.copies[0].wait_recv()
 
             @pl.loop(0, 4)
             def _(i):
                 y, x = i // 2, i % 2
-                total[y, x] = total[y, x] + self.pair[y, x]
+                mine = total[y, x] if self.outside else self.own[y, x, :, p.c]
+                total[y, x] = mine + self.pair[y, x]
 
             self.copies[1].start()
             self.copies[2].start()
@@ -473,13 +478,17 @@
         for i in (5, 6, 7):
             self.copies[i].wait_recv()
         p = self.place
-        value = total = self.total[p.y, p.x, p.z].astype(FULL)
+        value = self.total[p.y, p.x, p.z].astype(FULL)
         for d in range(3):
             value = value + self.last[d].astype(FULL)
         return value
 
+    def release(self):
+        self.copies[0].wait_send()
+        self.released = True
+
     def finish(self):
-        for copy in self.copies:
+        for copy in self.copies[1 if self.released else 0 :]:
             copy.wait_send()
 
 
@@ -975,36 +984,6 @@
     )(tokens, cotangent, starts, in_weight, out_weight, up_weight, down_weight, pack)
 
 
-def scatter_kernel(inputs, outputs, wide, tall, send, recv):
-    p = Place()
-    p.meet()
-    order = [8, 9, 10, 11, 4, 5, 6, 7, 3, 0, 1, 2]
-    chunks = []
-    places = []
-    for j in range(12):
-        if j < 8:
-            source = 0 if j < 3 else (1 if j == 3 else 2)
-            column = j if j < 3 else (0 if j == 3 else j - 4)
-            columns = pl.ds(column * 1024, 1024)
-            own, buffers, at = inputs[source].at[:, :, :, :, :, columns], wide, j
-        else:
-            source, columns, buffers, at = 3, pl.ds((j - 8) * 256, 256), tall, j - 8
-            own = inputs[3].at[:, :, :, :, :, columns]
-        chunks.append(Scatter(p, own, *[ref.at[at] for ref in buffers], send.at[j], recv.at[j]))
-        places.append((source, columns))
-    for tick in range(12 + 4):
-        for number in range(5):
-            if 0 <= tick - number < 12:
-                j = order[tick - number]
-                if number < 4:
-                    chunks[j].step(number)
-                else:
-                    source, columns = places[j]
-                    outputs[source][:, columns] = chunks[j].result()
-    for chunk in chunks:
-        chunk.finish()
-
-
 def scatter_buffers(count, rows, columns):
     half = rows // 2
     shapes = [
@@ -1019,26 +998,510 @@
     return [pltpu.VMEM((count, *shape), LOW) for shape in shapes]
 
 
-def scatter_all(*grads):
+class Sum:
+    def __init__(self, place, stages, landed, send, recv):
+        p = place
+        devices = [p.sibling, p.over_x, p.over_y, *p.along_z]
+        self.stages, self.landed = stages, landed
+        self.copies = [
+            remote(stages.at[min(i, 3)], landed.at[i], send.at[i], recv.at[i], device)
+            for i, device in enumerate(devices)
+        ]
+
+    def step(self, number):
+        stages, landed = self.stages, self.landed
+        if 1 <= number <= 3:
+            self.copies[number - 1].wait_recv()
+            stages[number] = stages[number - 1] + landed[number - 1]
+        if number < 3:
+            self.copies[number].start()
+        elif number == 3:
+            for i in (3, 4, 5):
+                self.copies[i].start()
+
+    def result(self):
+        for i in (3, 4, 5):
+            self.copies[i].wait_recv()
+        return (self.stages[3] + self.landed[3]) + (self.landed[4] + self.landed[5])
+
+    def finish(self):
+        for copy in self.copies:
+            copy.wait_send()
+
+
+def backward_kernel(inputs, outputs, tall, wide, scratch):
+    (
+        tokens_in,
+        cotangent_in,
+        starts,
+        in_full,
+        out_full,
+        up_full,
+        down_full,
+        grad_down_in,
+        heads_in,
+        mixed_in,
+        inverse_in,
+        middle_in,
+        slope_in,
+        memory_in,
+        sums_in,
+        gains_in,
+    ) = inputs
+    (
+        cotangent,
+        normed,
+        slab,
+        broad,
+        grad_middle,
+        inner,
+        mixed,
+        inverse,
+        memory,
+        sums,
+        gains,
+        mask,
+        mask_back,
+        parts,
+        done_in,
+        done_out,
+        done_up,
+        done_down,
+        stages,
+        landed,
+        outgoing,
+        incoming,
+        update,
+        key_update,
+        send,
+        recv,
+        sum_send,
+        sum_recv,
+        state_send,
+        state_recv,
+        local,
+        stream,
+        store,
+    ) = scratch
+    p = Place()
+    length, width = cotangent.shape
+
+    pairs = [
+        (cotangent_in, cotangent),
+        (slope_in, broad),
+        (middle_in, grad_middle),
+        (gains_in, gains),
+        (memory_in, memory),
+        (sums_in, sums),
+        (mixed_in, mixed),
+        (inverse_in, inverse),
+        (tokens_in, cotangent),
+    ]
+    pairs += [(heads_in.at[k], broad.at[:, pl.ds(1024 * k, 1024)]) for k in range(3)]
+    loads = [pltpu.make_async_copy(a, b, local.at[i]) for i, (a, b) in enumerate(pairs)]
+    slabs = [down_full.at[pl.ds(1024 * j, 1024), :] for j in range(4)]
+    slabs += [up_full.at[:, pl.ds(1024 * j, 1024)] for j in range(4)]
+    slabs += [out_full]
+    slabs += [in_full.at[:, pl.ds(1024 * j, 1024)] for j in range(3)]
+    slabs = [
+        pltpu.make_async_copy(source, slab.at[i % 2], stream.at[i]) for i, source in enumerate(slabs)
+    ]
+    order = [8, 9, 10, 11, 4, 5, 6, 7, 3, 0, 1, 2]
+    room = {4: 0, 5: 1, 6: 2, 7: 0, 3: 1, 0: 2, 1: 0, 2: 1}
+    chunks = []
+    for j in range(12):
+        if j < 8:
+            first, *others = [ref.at[j] for ref in wide]
+            buffers = [first, first, *others]
+            own = parts.at[room[j]]
+        else:
+            buffers = [ref.at[j - 8] for ref in tall]
+            own = grad_down_in.at[j - 8]
+        chunks.append(Scatter(p, own, *buffers, send.at[j], recv.at[j], j >= 8))
+
+    p.meet()
+    chunks[8].step(0)
+    for i in range(4):
+        loads[i].start()
+    slabs[0].start()
+    slabs[1].start()
+    for i in range(4, 8):
+        loads[i].start()
+    stores = []
+
+    def save(source, target):
+        copy = pltpu.make_async_copy(source, target, store.at[len(stores)])
+        copy.start()
+        stores.append(copy)
+
+    def event(position, number):
+        if not 0 <= position < 12:
+            return
+        j = order[position]
+        if number < 4:
+            if (j, number) != (8, 0):
+                chunks[j].step(number)
+            return
+        if j < 8:
+            target, k = (done_in, j) if j < 3 else ((done_out, 0) if j == 3 else (done_up, j - 4))
+            size = 1024
+        else:
+            target, k, size = done_down, j - 8, 256
+        where = outputs[0 if j < 3 else 1 if j == 3 else 2 if j < 8 else 3]
+        target[:, size * k : size * k + size] = chunks[j].result()
+        save(target.at[:, pl.ds(size * k, size)], where.at[:, pl.ds(size * k, size)])
+
+    images = Images(starts, p.seq, length)
+
+    def second_norm():
+        loads[2].wait()
+        loads[3].wait()
+
+        @pl.loop(0, length // 128)
+        def _(i):
+            rows = tile(i, 128)
+            value, _ = statistics(grad_middle[rows, :])
+            normed[rows, :] = (value * gains[2:3, :] + gains[3:4, :]).astype(LOW)
+
+    def active_gradient(j):
+        if j == 0:
+            loads[0].wait()
+            loads[1].wait()
+        slabs[j].wait()
+
+        @pl.loop(0, 4)
+        def _(i):
+            columns = pl.ds(pl.multiple_of(1024 * j + 256 * i, 256), 256)
+            value = across(cotangent[...], slab[j % 2, tile(i, 256), :])
+            broad[:, columns] = (value * broad[:, columns].astype(FULL)).astype(LOW)
+
+        slabs[j + 2].start()
+
+    def weight_gradient(j, left, right):
+        at = room[j]
+
+        @pl.loop(0, 4)
+        def _(i):
+            value = down_rows(left(tile(i, 256)), right()).astype(LOW)
+            parts[at, i // 2, i % 2] = value.reshape(4, 2, 32, 1024)
+
+    def up_gradient(j):
+        if j == 3:
+            chunks[4].release()
+        weight_gradient(
+            4 + j,
+            lambda columns: normed[:, columns],
+            lambda: broad[:, 1024 * j : 1024 * j + 1024],
+        )
+        if j == 3:
+            for k in range(9, 12):
+                loads[k].start()
+
+    def inner_gradient(first, j):
+        slabs[first + j].wait()
+
+        @pl.loop(0, 4)
+        def _(i):
+            columns = tile(i, 256)
+            value = across(
+                broad[:, 1024 * j : 1024 * j + 1024], slab[(first + j) % 2, columns, :]
+            )
+            if j > 0:
+                value = value + inner[:, columns]
+            inner[:, columns] = value
+
+        if first + j + 2 < 12:
+            slabs[first + j + 2].start()
+
+    def norm_gradient(rows, values, gain):
+        unit, scale = statistics(values)
+        given = inner[rows, :]
+        scaled = given * gain
+        one = jnp.mean(scaled, axis=-1, keepdims=True)
+        two = jnp.mean(scaled * unit, axis=-1, keepdims=True)
+        return scale * (scaled - one - unit * two), given * unit, given
+
+    def fold(values):
+        return jnp.sum(values, axis=0, keepdims=True)
+
+    def middle_gradient():
+        stages[0] = jnp.zeros((8, width), FULL)
+
+        @pl.loop(0, length // 128)
+        def _(i):
+            rows = tile(i, 128)
+            value, gain, shift = norm_gradient(rows, grad_middle[rows, :], gains[2:3, :])
+            stages[0, 2:3, :] += fold(gain)
+            stages[0, 3:4, :] += fold(shift)
+            value = value + cotangent[rows, :].astype(FULL)
+            grad_middle[rows, :] = value
+            cotangent[rows, :] = value.astype(LOW)
+
+    def output_gradient():
+        loads[6].wait()
+        chunks[5].release()
+        weight_gradient(
+            3, lambda columns: mixed[:, columns].astype(LOW), lambda: cotangent[...]
+        )
+        loads[8].start()
+
+    def mixed_gradient():
+        slabs[8].wait()
+
+        @pl.loop(0, 4)
+        def _(i):
+            columns = tile(i, 256)
+            inner[:, columns] = across(cotangent[...], slab[0, columns, :])
+
+        slabs[10].start()
+
+    state = [
+        remote(outgoing, incoming.at[d], state_send.at[d], state_recv.at[d], device)
+        for d, device in enumerate(p.preceding)
+    ]
+
+    def numerator_gradient():
+        for i in (4, 5, 7, 9, 10, 11):
+            loads[i].wait()
+        blocks = own_block()
+        doubled = jnp.concatenate([blocks, blocks], axis=0)
+
+        @pl.loop(0, 8)
+        def _(i):
+            lanes = tile(i, 128)
+            given, over = inner[:, lanes], inverse[:, lanes]
+            numerator = (given * over).astype(LOW)
+            each = given * mixed[:, lanes]
+            high = each.astype(LOW)
+            rest = (each - high.astype(FULL)).astype(LOW)
+            slant = product(jnp.concatenate([high, rest], axis=1), doubled) * over * -1.0
+            mixed[:, lanes] = slant
+            broad[:, pl.ds(pl.multiple_of(3072 + 128 * i, 128), 128)] = numerator
+            kept = broad[:, lanes].astype(FULL) * images.keep
+            square = down_rows(kept.astype(LOW), numerator)
+            outgoing[i, 0:HEAD] = pack_pair(square).astype(LOW)
+            total = fold(kept * slant)
+            outgoing[i, HEAD : HEAD + 16] = jnp.broadcast_to(total, (16, 128)).astype(LOW)
+
+        for copy in state:
+            copy.start()
+        mask[...] = same_mask(images, length, length, False)
+        mask_back[...] = same_mask(images, length, length, True)
+
+    def enter():
+        for copy in state:
+            copy.wait_recv()
+        flag = jnp.where(p.seq == 7, 0.0, images.flag_after)
+
+        @pl.loop(0, 8)
+        def _(i):
+            value = incoming[0, i].astype(FULL) + flag * incoming[1, i].astype(FULL)
+            update[i] = value[0:HEAD].astype(LOW)
+            key_update[i] = value[HEAD : HEAD + 8]
+
+    def attend(begin, end):
+        if begin == 0:
+            enter()
+        if end == 8:
+            first_norm()
+        first = head_lanes(length)
+        lane = lax.broadcasted_iota(jnp.int32, (length, 128), 1)
+        ones = jnp.ones((length, 128), LOW)
+        zero = jnp.zeros((length, 128), LOW)
+        half = length // 2
+
+        @pl.loop(begin, end)
+        def _(i):
+            at = [pl.ds(pl.multiple_of(1024 * k + 128 * i, 128), 128) for k in range(4)]
+            query, key, value, numerator = [broad[:, lanes] for lanes in at]
+            slant = mixed[:, at[0]]
+            high = slant.astype(LOW)
+            rest = (slant - high.astype(FULL)).astype(LOW)
+            right = jnp.concatenate([value, ones], axis=1)
+            grads = []
+            for h in range(2):
+                mine = first if h == 0 else ~first
+                own_query = jnp.where(mine, query, zero)
+                left = jnp.concatenate(
+                    [
+                        jnp.where(mine, numerator, zero),
+                        jnp.where(
+                            lane == HEAD * h, high, jnp.where(lane == HEAD * h + 1, rest, zero)
+                        ),
+                    ],
+                    axis=1,
+                )
+                upper = across(left[:half], right[:half]).astype(LOW) * mask[:half, :half]
+                lower = across(left[half:], right).astype(LOW) * mask[half:, :]
+                for_query = jnp.concatenate([product(upper, key[:half]), product(lower, key)], axis=0)
+                upper = across(right[:half], left).astype(LOW) * mask_back[:half, :]
+                lower = across(right[half:], left[half:]).astype(LOW) * mask_back[half:, half:]
+                for_key = jnp.concatenate(
+                    [product(upper, query), product(lower, query[half:])], axis=0
+                )
+                upper = across(key[:half], own_query).astype(LOW) * mask_back[:half, :]
+                lower = across(key[half:], own_query[half:]).astype(LOW) * mask_back[half:, half:]
+                for_value = jnp.concatenate(
+                    [product(upper, numerator), product(lower, numerator[half:])], axis=0
+                )
+                grads.append((for_query, for_key, for_value))
+            for_query, for_key, for_value = [
+                jnp.where(first, one, two) for one, two in zip(*grads, strict=True)
+            ]
+            keep, tail = images.keep, images.tail
+            for_query = for_query + keep * (
+                across(numerator, unpack_pair(memory[i])) + slant * sums[i, 0:1]
+            )
+            square = unpack_pair(update[i])
+            for_key = for_key + tail * (across(value, square) + key_update[i, 0:1])
+            for_value = for_value + product(key * tail.astype(LOW), square)
+            broad[:, at[0]] = (for_query * jnp.minimum(query.astype(FULL), 1.0)).astype(LOW)
+            broad[:, at[1]] = (for_key * jnp.minimum(key.astype(FULL), 1.0)).astype(LOW)
+            broad[:, at[2]] = for_value.astype(LOW)
+
+    def first_norm():
+        loads[8].wait()
+
+        @pl.loop(0, length // 128)
+        def _(i):
+            rows = tile(i, 128)
+            value, _ = statistics(cotangent[rows, :].astype(FULL))
+            normed[rows, :] = (value * gains[0:1, :] + gains[1:2, :]).astype(LOW)
+
+    def in_gradient(j):
+        chunks[(6, 7, 3)[j]].release()
+        weight_gradient(
+            j,
+            lambda columns: normed[:, columns],
+            lambda: broad[:, 1024 * j : 1024 * j + 1024],
+        )
+
+    total = Sum(p, stages, landed, sum_send, sum_recv)
+
+    def token_gradient():
+        @pl.loop(0, length // 128)
+        def _(i):
+            rows = tile(i, 128)
+            value, gain, shift = norm_gradient(rows, cotangent[rows, :].astype(FULL), gains[0:1, :])
+            stages[0, 0:1, :] += fold(gain)
+            stages[0, 1:2, :] += fold(shift)
+            grad_middle[rows, :] += value
+
+        save(grad_middle, outputs[4])
+        total.step(0)
+
+    do = functools.partial
+    work = {
+        0: [second_norm],
+        1: [do(active_gradient, 0), do(active_gradient, 1), do(active_gradient, 2)],
+        2: [do(active_gradient, 3), do(up_gradient, 0), do(up_gradient, 1)],
+        3: [do(up_gradient, 2), do(inner_gradient, 4, 0), do(inner_gradient, 4, 1)],
+        4: [do(inner_gradient, 4, 2), do(inner_gradient, 4, 3), middle_gradient],
+        5: [do(up_gradient, 3), mixed_gradient],
+        6: [output_gradient, numerator_gradient],
+        7: [do(attend, 0, 2), do(attend, 2, 4), do(attend, 4, 5)],
+        8: [do(attend, 5, 7), do(attend, 7, 8), do(in_gradient, 0)],
+        9: [do(in_gradient, 1), do(in_gradient, 2), do(inner_gradient, 9, 0)],
+        10: [
+            do(inner_gradient, 9, 1),
+            do(inner_gradient, 9, 2),
+            token_gradient,
+        ],
+        11: [do(total.step, 1), do(total.step, 2), do(total.step, 3)],
+    }
+    for tick in range(12 + 4):
+        todo = work.get(tick, []) + [lambda: None] * 3
+        event(tick, 0)
+        event(tick - 1, 1)
+        todo[0]()
+        event(tick - 2, 2)
+        todo[1]()
+        event(tick - 3, 3)
+        event(tick - 4, 4)
+        todo[2]()
+    total_value = total.result()
+    landed[0] = total_value
+    group = (p.dp * 8 + p.seq) // 4
+    mine = landed[0, :, tile(group, 128)]
+    mine = pltpu.roll(mine, (128 - 32 * (p.seq % 4)) % 128, 1)
+    for k in range(4):
+        outputs[5 + k][...] = mine[k : k + 1, 0:32]
+    total.finish()
+    for copy in state:
+        copy.wait_send()
+    for chunk in chunks:
+        chunk.finish()
+    for copy in stores:
+        copy.wait()
+
+
+def backward_pass(*inputs):
+    length, width = inputs[0].shape
+    shape = jax.ShapeDtypeStruct
+    vmem = pltpu.VMEM
+    tall = scatter_buffers(4, 128, 256)
+    wide = scatter_buffers(8, 32, 1024)[1:]
+
     def body(*refs):
-        scatter_kernel(refs[:4], refs[4:8], refs[8:15], refs[15:22], *refs[22:])
+        backward_kernel(refs[:16], refs[16:25], refs[25:32], refs[32:38], refs[38:])
 
     return pl.pallas_call(
         body,
         out_shape=[
-            jax.ShapeDtypeStruct(shape, FULL)
-            for shape in ((32, 3072), (32, 1024), (32, 4096), (128, 1024))
+            shape((32, 3072), FULL),
+            shape((32, 1024), FULL),
+            shape((32, 4096), FULL),
+            shape((128, 1024), FULL),
+            shape((length, width), FULL),
+            *[shape((1, 32), FULL)] * 4,
         ],
-        in_specs=[pl.BlockSpec(memory_space=pl.ANY)] * 4,
-        out_specs=[pl.BlockSpec(memory_space=pltpu.VMEM)] * 4,
-        scratch_shapes=scatter_buffers(8, 32, 1024)
-        + scatter_buffers(4, 128, 256)
-        + [pltpu.SemaphoreType.DMA((12, 9)), pltpu.SemaphoreType.DMA((12, 8))],
+        in_specs=[
+            pl.BlockSpec(memory_space=pltpu.SMEM if i == 2 else pl.ANY) for i in range(16)
+        ],
+        out_specs=[pl.BlockSpec(memory_space=pl.ANY)] * 5
+        + [pl.BlockSpec(memory_space=pltpu.VMEM)] * 4,
+        scratch_shapes=[
+            *tall,
+            *wide,
+            vmem((length, width), LOW),
+            vmem((length, width), LOW),
+            vmem((2, width, width), LOW),
+            vmem((length, 4 * width), LOW),
+            vmem((length, width), FULL),
+            vmem((length, width), FULL),
+            vmem((length, width), FULL),
+            vmem((length, width), FULL),
+            vmem((8, HEAD, 128), LOW),
+            vmem((8, 8, 128), FULL),
+            vmem((16, width), FULL),
+            vmem((length, length), LOW),
+            vmem((length, length), LOW),
+            vmem((3, 2, 2, 4, 2, 32, 1024), LOW),
+            vmem((32, 3072), FULL),
+            vmem((32, 1024), FULL),
+            vmem((32, 4096), FULL),
+            vmem((128, 1024), FULL),
+            vmem((4, 8, width), FULL),
+            vmem((6, 8, width), FULL),
+            vmem((8, HEAD + 16, 128), LOW),
+            vmem((2, 8, HEAD + 16, 128), LOW),
+            vmem((8, HEAD, 128), LOW),
+            vmem((8, 8, 128), FULL),
+            pltpu.SemaphoreType.DMA((12, 9)),
+            pltpu.SemaphoreType.DMA((12, 8)),
+            pltpu.SemaphoreType.DMA((6,)),
+            pltpu.SemaphoreType.DMA((6,)),
+            pltpu.SemaphoreType.DMA((2,)),
+            pltpu.SemaphoreType.DMA((2,)),
+            pltpu.SemaphoreType.DMA((12,)),
+            pltpu.SemaphoreType.DMA((12,)),
+            pltpu.SemaphoreType.DMA((13,)),
+        ],
         compiler_params=pltpu.CompilerParams(
-            collective_id=1, has_side_effects=True, vmem_limit_bytes=60 << 20
+            collective_id=1, has_side_effects=True, vmem_limit_bytes=62 << 20
         ),
-        name="scatter_gradients",
-    )(*[grad.reshape(2, 2, 4, 2, grad.shape[0] // 32, grad.shape[1]) for grad in grads])
+        name="backward_pass",
+    )(*inputs)
 
 
 def on_device(
@@ -1054,38 +1517,10 @@
     second_shift,
     cotangent,
 ):
-    local_len = tokens.shape[1]
-    model_width = tokens.shape[2]
-    head_count = model_width // HEAD
-    block_count = local_len // BLOCK
-    block_shape = (block_count, BLOCK, head_count, HEAD)
-    zero_low = jnp.zeros((), jnp.bfloat16)
-    input_tokens = tokens[0].astype(jnp.float32)
-    first_pos = lax.axis_index("seq") * local_len
-    positions = first_pos + jnp.arange(local_len, dtype=jnp.int32)
-    pack_starts = starts[0]
-    image_ids = jnp.sum((pack_starts[None, :] <= positions[:, None]).astype(jnp.int32), axis=1) - 1
-    before_id = jnp.sum((pack_starts <= first_pos - 1).astype(jnp.int32)) - 1
-    causal = jnp.arange(BLOCK)[:, None] >= jnp.arange(BLOCK)[None, :]
     mine = lax.axis_index("dp") * 8 + lax.axis_index("seq")
     pack = jnp.stack([first_gain, first_shift, second_gain, second_shift]).astype(FULL)
     pack = jnp.roll(jnp.pad(pack, ((0, 12), (0, 96))), 32 * (mine % 4), axis=1).astype(LOW)
-    (
-        in_full,
-        out_full,
-        up_full,
-        down_full,
-        grad_down,
-        result,
-        heads,
-        mixed,
-        inverse,
-        middle_tokens,
-        slope,
-        memory,
-        sums,
-        gains,
-    ) = forward_pass(
+    in_full, out_full, up_full, down_full, grad_down, result, *saved = forward_pass(
         tokens[0],
         cotangent[0],
         starts,
@@ -1095,160 +1530,19 @@
         down_projection_weight,
         pack,
     )
-    result_tokens = result.reshape(1, local_len, model_width)
-    in_full, out_full = in_full.reshape(1024, 3072), out_full.reshape(1024, 1024)
-    up_full, down_full = up_full.reshape(1024, 4096), down_full.reshape(4096, 1024)
-    gain_one, shift_one, gain_two, shift_two = gains[0], gains[1], gains[2], gains[3]
-    normed_low = layer_norm(input_tokens, gain_one, shift_one).astype(LOW)
-    projected_tokens = jnp.dot(normed_low, in_full, preferred_element_type=jnp.float32)
-    queries = projected_tokens[:, :model_width]
-    keys_raw = projected_tokens[:, model_width : 2 * model_width]
-    feat_query, feat_key, value_low = heads[0].reshape(block_shape), heads[1].reshape(block_shape), heads[2].reshape(block_shape)
-    last_id = image_ids[-1]
-    tail_mask = image_ids == last_id
-    keep_list = [image_ids == before_id]
-    tail_list = [tail_mask]
-    flag_list = [(last_id == before_id).astype(jnp.float32)]
-    same_list = [causal & (image_ids[:, None] == image_ids[None, :])]
-    identity = (
-        jnp.ones((), jnp.float32),
-        jnp.zeros((head_count, HEAD, HEAD), jnp.float32),
-        jnp.zeros((head_count, HEAD), jnp.float32),
-    )
-    memory_list = [jnp.transpose(memory.reshape(8, HEAD, 2, HEAD), (0, 2, 1, 3)).reshape(16, HEAD, HEAD)]
-    keysum_list = [sums[:, 0].reshape(16, HEAD)]
-    denominator = 1.0 / inverse.reshape(512, 16, 64)
-    numer_list = [mixed.reshape(512, 16, 64) * denominator]
-    denom_list = [denominator[:, :, 0]]
-    mixed_low = mixed.astype(LOW)
-    normed_two_low = layer_norm(middle_tokens, gain_two, shift_two).astype(jnp.bfloat16)
-    grad_out = cotangent[0].astype(jnp.float32)
-    grad_out_low = cotangent[0]
-    d_active = cols_product(grad_out_low, down_full)
-    g_upper = (slope.astype(FULL) * d_active).astype(jnp.bfloat16)
-    grad_up = rows_product(normed_two_low, g_upper)
-    d_normed_two = cols_product(g_upper, up_full)
-    norm_value, norm_back = jax.vjp(layer_norm, middle_tokens, gain_two, shift_two)
-    middle_part, grad_gain_two, grad_shift_two = norm_back(d_normed_two)
-    g_middle = grad_out + middle_part
-    g_middle_low = g_middle.astype(jnp.bfloat16)
-    grad_out_weight = rows_product(mixed_low, g_middle_low)
-    d_mixed = cols_product(g_middle_low, out_full).reshape(block_shape)
-    block_number = 0
-    query_block = feat_query[block_number]
-    denominator = denom_list[block_number]
-    g_numerator = (d_mixed[block_number] / denominator[:, :, None]).astype(jnp.bfloat16)
-    g_denominator = -jnp.sum(d_mixed[block_number] * numer_list[block_number], axis=2) / (
-        denominator * denominator
-    )
-    kept_query = jnp.where(keep_list[block_number][:, None, None], query_block, zero_low)
-    gnum_list = [g_numerator]
-    gden_list = [g_denominator]
-    local_list = [
-        jnp.einsum("the,thf->hef", kept_query, g_numerator, preferred_element_type=jnp.float32)
-    ]
-    localkey_list = [jnp.sum(kept_query.astype(jnp.float32) * g_denominator[:, :, None], axis=0)]
-    combined = identity
-    for block_number in reversed(range(block_count)):
-        combined = combine(
-            combined,
-            (flag_list[block_number], local_list[block_number], localkey_list[block_number]),
-        )
-    leaving = prefix(combined, "seq", combine, identity, True)
-    g_memory = leaving[1]
-    g_key_sum = leaving[2]
-    gq_list = []
-    gk_list = []
-    gv_list = []
-    for block_number in reversed(range(block_count)):
-        query_block = feat_query[block_number]
-        key_block = feat_key[block_number]
-        value_block = value_low[block_number]
-        keep_float = keep_list[block_number].astype(jnp.float32)
-        tail_float = tail_list[block_number].astype(jnp.float32)
-        g_numerator = gnum_list[block_number]
-        g_denominator = gden_list[block_number]
-        g_update = g_memory.astype(jnp.bfloat16)
-        raw_scores = jnp.einsum(
-            "the,jhe->htj", query_block, key_block, preferred_element_type=jnp.float32
-        )
-        scores_low = jnp.where(same_list[block_number][None], raw_scores, 0.0).astype(jnp.bfloat16)
-        g_scores = (
-            jnp.einsum("thf,jhf->htj", g_numerator, value_block, preferred_element_type=jnp.float32)
-            + jnp.transpose(g_denominator)[:, :, None]
-        )
-        g_scores_low = jnp.where(
-            same_list[block_number][None], g_scores.astype(jnp.bfloat16), zero_low
-        )
-        query_grad = jnp.einsum(
-            "htj,jhe->the", g_scores_low, key_block, preferred_element_type=jnp.float32
-        )
-        query_grad = query_grad + keep_float[:, None, None] * (
-            jnp.einsum(
-                "thf,hef->the",
-                g_numerator,
-                memory_list[block_number],
-                preferred_element_type=jnp.float32,
-            )
-            + g_denominator[:, :, None] * keysum_list[block_number][None]
-        )
-        key_grad = jnp.einsum(
-            "htj,the->jhe", g_scores_low, query_block, preferred_element_type=jnp.float32
-        )
-        key_grad = key_grad + tail_float[:, None, None] * (
-            jnp.einsum("jhf,hef->jhe", value_block, g_update, preferred_element_type=jnp.float32)
-            + g_key_sum[None]
-        )
-        tail_key = jnp.where(tail_list[block_number][:, None, None], key_block, zero_low)
-        value_grad = jnp.einsum(
-            "htj,thf->jhf", scores_low, g_numerator, preferred_element_type=jnp.float32
-        )
-        value_grad = value_grad + jnp.einsum(
-            "jhe,hef->jhf", tail_key, g_update, preferred_element_type=jnp.float32
-        )
-        gq_list.append(query_grad)
-        gk_list.append(key_grad)
-        gv_list.append(value_grad)
-        g_memory = local_list[block_number] + flag_list[block_number] * g_memory
-        g_key_sum = localkey_list[block_number] + flag_list[block_number] * g_key_sum
-    d_feat_query = jnp.concatenate(gq_list[::-1], axis=0).reshape(local_len, model_width)
-    d_feat_key = jnp.concatenate(gk_list[::-1], axis=0).reshape(local_len, model_width)
-    d_value = jnp.concatenate(gv_list[::-1], axis=0).reshape(local_len, model_width)
-    query_value, query_back = jax.vjp(feature, queries)
-    key_value, key_back = jax.vjp(feature, keys_raw)
-    g_projected = jnp.concatenate(
-        [query_back(d_feat_query)[0], key_back(d_feat_key)[0], d_value], axis=1
-    ).astype(jnp.bfloat16)
-    grad_in_weight = rows_product(normed_low, g_projected)
-    d_normed = cols_product(g_projected, in_full)
-    first_value, first_back = jax.vjp(layer_norm, input_tokens, gain_one, shift_one)
-    input_part, grad_gain_one, grad_shift_one = first_back(d_normed)
-    grad_tokens = (g_middle + input_part).reshape(1, local_len, model_width)
-    weights = scatter_all(
-        grad_in_weight.astype(LOW),
-        grad_out_weight.astype(LOW),
-        grad_up.astype(LOW),
-        jnp.moveaxis(grad_down, 0, 5).reshape(4096, 1024),
-    )
-    summed = (
-        *weights,
-        lax.psum_scatter(grad_gain_one, ("dp", "seq"), scatter_dimension=0, tiled=True),
-        lax.psum_scatter(grad_shift_one, ("dp", "seq"), scatter_dimension=0, tiled=True),
-        lax.psum_scatter(grad_gain_two, ("dp", "seq"), scatter_dimension=0, tiled=True),
-        lax.psum_scatter(grad_shift_two, ("dp", "seq"), scatter_dimension=0, tiled=True),
-    )
-    return (
-        result_tokens,
-        grad_tokens,
-        summed[0],
-        summed[1],
-        summed[2],
-        summed[3],
-        summed[4],
-        summed[5],
-        summed[6],
-        summed[7],
-    )
+    grads = backward_pass(
+        tokens[0],
+        cotangent[0],
+        starts,
+        in_full.reshape(1024, 3072),
+        out_full.reshape(1024, 1024),
+        up_full.reshape(1024, 4096),
+        down_full.reshape(4096, 1024),
+        grad_down,
+        *saved,
+    )
+    vectors = [grad.reshape(32) for grad in grads[5:]]
+    return (result[None], grads[4][None], *grads[:4], *vectors)
 
 
 def solution(mesh):

time: 528 us -> 275 us (0.52); the launches traced: 518 us -> 275 us
  matrix products: 84.2 us -> 0 us
  blocking collectives: 69.7 us -> 0 us
  local copies, waits for them, and re-layouts: 53.2 us -> 8.31 us
  other arithmetic: 33.1 us -> 1.4 us
  between operations: 16.3 us -> 0.77 us
  Pallas kernels: 256 us -> 264 us
  loops' own time: 5.8 us -> 0 us
    dot_general x16 -> x0, matrix products: 84.2 us -> none  [the longest x4 23.5 us: cols_product(): lax.dot_general(factor_one, factor_two, (((1,), (1,)), ((), ())), preferr...]
    unnamed x2 -> x0, blocking collectives: 55.5 us -> none
    all_gather x1 -> x0, blocking collectives: 14.2 us -> none  [prefix(): lax.all_gather(part.astype(kind), axis)]
    reduce_sum x9 -> x0, other arithmetic: 12.5 us -> none  [the longest x2 4.08 us: layer_norm(): spread = jnp.mean(centred * centred, axis=-1, keepdims=True)]
    select_n x16 -> x0, other arithmetic: 10.3 us -> none  [lap(): return jax.tree.map(lambda a, b: jnp.where(reached, a, b), new, before)]
    slice x8 -> x0, local copies, waits for them, and re-layouts: 9.01 us -> none  [the longest x2 3.19 us: on_device(): heads[2].reshape(block_shape)]
    pallas_call x1, Pallas kernels: 121 us -> 130 us  [backward_pass(): pl.pallas_call(body, out_shape=[shape((32, 3072), FULL), shape((32, 1024)...]
    reshape x3 -> x0, local copies, waits for them, and re-layouts: 8.45 us -> none  [the longest x1 3.11 us: on_device(): jnp.concatenate(gk_list[::-1], axis=0).reshape(local_len, model_width)]
  transfers between devices with their start and end apart: 1 -> 0, of which waited for: 0 -> 0; matrix products, arithmetic and copies ran while one was open for 14% -> 0% of each run, Pallas kernels for 0% -> 0%
where the time goes in v3:
time: 275 us
  Pallas kernels  264 us (96%)
  local copies, waits for them, and re-layouts  8.31 us (3%)
    pallas_call x1, Pallas kernels, forward_pass(): pl.pallas_call(body, out_shape=[block(32, 3072), block(32, 1024), block(3...  135 us
    pallas_call x1, Pallas kernels, backward_pass(): pl.pallas_call(body, out_shape=[shape((32, 3072), FULL), shape((32, 1024)...  130 us
    unnamed x30, local copies, waits for them, and re-layouts  8.31 us

profile of v3, /device:TPU:0, one launch (start us, length us, event | category | flops | bytes accessed | tf_op | source)
XLA Modules:
  0.0 275.0 jit_solution(17289455256268718804)
XLA Ops:
  0.7 0.7 fusion.9
  1.4 0.7 convert_convert_fusion.refs_7_
  2.1 134.7 %forward_pass.1 = (bf16[2,2,4,2,32,3072]{5,4,3,2,1,0:T(8,128)(2,1)}, bf16[2,2,4,2,32,1024]{5,4,3,2,1,0:T(8,128)(2,1)}, bf16[2,2,4,2,32,4096]{5,4,3,2,1,0:T(8,128...) custom-call(bf16[512,1024]{1,0:T(8,128)(2,1)} %bitcast.19, ...), custom_call_target="tpu_custom_call" | custom-call | tf_op jit(solution)/shard_map/forward_pass/pallas_call | solution.py:927
  136.8 0.0 copy-start.1
  136.8 129.8 %backward_pass.1 = (f32[32,3072]{1,0:T(8,128)}, f32[32,1024]{1,0:T(8,128)}, f32[32,4096]{1,0:T(8,128)}, f32[128,1024]{1,0:T(8,128)}, f32[512,1024]{1,0:T(8,128)}...) custom-call(bf16[512,1024]{1,0:T(8,128)(2,1)} %bitcast.20, ...), custom_call_target="tpu_custom_call" | custom-call | tf_op jit(solution)/shard_map/backward_pass/pallas_call | solution.py:1448
  266.6 0.0 copy-start
  266.6 0.0 copy-done.1
  266.6 0.0 copy-start.4
  266.6 0.0 copy-start.5
  266.6 0.0 copy-start.3
  266.6 1.0 copy.31
  267.6 0.9 copy-done
  268.6 0.0 copy-start.2
  268.6 0.0 copy-start.9
  268.6 0.0 copy-start.8
  268.6 0.0 copy-start.7
  268.6 0.0 copy-start.6
  268.6 1.3 copy.32
  269.9 0.0 copy-done.4
  269.9 0.7 copy.33
  270.7 0.0 copy-done.5
  270.7 0.7 copy.34
  271.3 0.0 copy-done.3
  271.3 0.8 copy.35
  272.1 0.0 copy-done.2
  272.1 0.8 copy.36
  272.9 0.0 copy-done.9
  272.9 0.5 copy.37
  273.4 0.0 copy-done.8
  273.4 0.5 copy.38
  273.9 0.0 copy-done.7
  273.9 0.5 copy.39
  274.5 0.0 copy-done.6
  274.5 0.5 copy.40
Async XLA Ops:
  136.8 129.9 %copy-start.1 = (bf16[512,1024]{1,0:T(8,128)(2,1)S(1)}, bf16[512,1024]{1,0:T(8,128)(2,1)}, u32[]{:S(2)}) copy-start(bf16[512,1024]{1,0:T(8,128)(2,1)} %get-tuple-element.33) | copy-start | bytes 3145732
  266.6 2.0 copy-start
  266.6 3.3 %copy-start.4 = (f32[32,3072]{1,0:T(8,128)S(1)}, f32[32,3072]{1,0:T(8,128)}, u32[]{:S(2)}) copy-start(f32[32,3072]{1,0:T(8,128)} %get-tuple-element.68) | copy-start | bytes 1179652
  266.6 4.0 %copy-start.5 = (f32[32,1024]{1,0:T(8,128)S(1)}, f32[32,1024]{1,0:T(8,128)}, u32[]{:S(2)}) copy-start(f32[32,1024]{1,0:T(8,128)} %get-tuple-element.69) | copy-start | bytes 393220
  266.6 4.7 %copy-start.3 = (f32[32,4096]{1,0:T(8,128)S(1)}, f32[32,4096]{1,0:T(8,128)}, u32[]{:S(2)}) copy-start(f32[32,4096]{1,0:T(8,128)} %get-tuple-element.70) | copy-start | bytes 1572868
  268.6 3.5 %copy-start.2 = (f32[128,1024]{1,0:T(8,128)S(1)}, f32[128,1024]{1,0:T(8,128)}, u32[]{:S(2)}) copy-start(f32[128,1024]{1,0:T(8,128)} %get-tuple-element.71) | copy-start | bytes 1572868
  268.6 4.3 %copy-start.9 = (f32[1,32]{1,0:T(1,128)S(1)}, f32[1,32]{1,0:T(1,128)}, u32[]{:S(2)}) copy-start(f32[1,32]{1,0:T(1,128)} %get-tuple-element.52) | copy-start | bytes 388
  268.6 4.9 %copy-start.8 = (f32[1,32]{1,0:T(1,128)S(1)}, f32[1,32]{1,0:T(1,128)}, u32[]{:S(2)}) copy-start(f32[1,32]{1,0:T(1,128)} %get-tuple-element.53) | copy-start | bytes 388
  268.6 5.4 %copy-start.7 = (f32[1,32]{1,0:T(1,128)S(1)}, f32[1,32]{1,0:T(1,128)}, u32[]{:S(2)}) copy-start(f32[1,32]{1,0:T(1,128)} %get-tuple-element.54) | copy-start | bytes 388
  268.6 5.9 %copy-start.6 = (f32[1,32]{1,0:T(1,128)S(1)}, f32[1,32]{1,0:T(1,128)}, u32[]{:S(2)}) copy-start(f32[1,32]{1,0:T(1,128)} %get-tuple-element.55) | copy-start | bytes 388
